TPU v7x, 32 devices: a whole 2x2x4 slice. The times are simulated.
32 devices in a mesh: dist: 8 (over y, x, core), mem: 4 (over z).
Axes of the slice: x: 2, y: 2, z: 4, core: 2. Of those that a mesh axis runs over, the one named last changes fastest.
Arguments:
- anomalies: bfloat16 [64, 2048, 512], P('dist', None, 'mem'), may hold values from -6 to 6
- innovations: bfloat16 [64, 256, 512], P('dist', None, 'mem'), may hold values from -6 to 6
- obs_var: bfloat16 [64, 256], P('dist'), may hold values from 0.25 to 2
- node_pos: bfloat16 [2, 64, 2048], P(None, 'dist'), may hold values from 0 to 1
- obs_node: int32 [64, 256], P('dist'), may hold values from 0 to 2047
- obs_count: int32 [64], P('dist'), may hold values from 64 to 256, as said below
- in_radius: int32 [64, 7], P('dist'), may hold values from 0 to 1, as said below
Outputs:
- increment: float32 [64, 2048, 512], P('dist', 'mem')
Inputs may be any that keep to these rules, and one draw needn't show every extreme that they name: `obs_count`: every district has at least 64 observations in use, and some district has all 256. `in_radius`: slot 3 (the district itself) is always 1; the ones of a district form a band of slots around it; slots naming a district outside 0 to 63 are 0; some district is paired with all districts up to 3 away.
All inputs are finite; a program needn't handle non-finite values.
Results may differ from a plain program's by a relative error of at most 0.0029.
Values may be sent and summed in bfloat16 or wider, within the bound.
No kernel may reach another device: no remote copies, remote signals or barrier semaphores. Data moves between devices by JAX's collectives and lax.ppermute only.
A program may use at most 192 MiB of HBM per device.

v0:
```python
import functools
import jax
import jax.numpy as jnp
from jax import lax
from jax.experimental import pallas as pl
from jax.experimental.pallas import tpu as pltpu
from jax.sharding import PartitionSpec as P

BF = jnp.bfloat16
F32 = jnp.float32
VMEM_LIMIT = 62 * 1024 * 1024
SPREAD_COST = 30
PACE = 1.0
WHOLE = pl.BlockSpec(memory_space=pltpu.HBM)
CHUNKS = (5, 3)


def params(**more):
    return pltpu.CompilerParams(vmem_limit_bytes=VMEM_LIMIT, **more)


def cost(length):
    nominal = int(length * PACE * 3.69e6)
    return pl.CostEstimate(flops=nominal * 312, bytes_accessed=nominal, transcendentals=0)


def pick_kernel(node_ref, table_ref, pos_ref, *refs):
    obs_ref, xy_ref = refs[-2:]
    slots, nodes = node_ref.shape[1], table_ref.shape[1]
    here = lax.broadcasted_iota(jnp.int32, (slots, nodes), 1) == node_ref[0]
    hot = jnp.where(here, 1.0, 0.0).astype(BF)
    obs_ref[0] = jnp.dot(hot, table_ref[0], preferred_element_type=F32).astype(BF)
    xy_ref[0] = lax.dot_general(
        pos_ref[0], hot, (((1,), (1,)), ((), ())), preferred_element_type=F32
    ).astype(BF)


def pick(anomalies, obs_node, pos, after):
    count, nodes, width = anomalies.shape
    slots = obs_node.shape[1]
    return pl.pallas_call(
        pick_kernel,
        grid=(count,),
        in_specs=[
            pl.BlockSpec((1, slots, 1), lambda d: (d, 0, 0)),
            pl.BlockSpec((1, nodes, width), lambda d: (d, 0, 0)),
            pl.BlockSpec((1, 2, nodes), lambda d: (d, 0, 0)),
            *[WHOLE] * len(after),
        ],
        out_specs=[
            pl.BlockSpec((1, slots, width), lambda d: (d, 0, 0)),
            pl.BlockSpec((1, 2, slots), lambda d: (d, 0, 0)),
        ],
        out_shape=[
            jax.ShapeDtypeStruct((count, slots, width), BF),
            jax.ShapeDtypeStruct((count, 2, slots), BF),
        ],
        compiler_params=params(),
        cost_estimate=cost(7),
        name="pick",
    )(obs_node[:, :, None], anomalies, pos, *after)


def taper_kernel(reach, first, *refs):
    flags_ref, node_ref, meta_ref = refs[:3]
    out_ref, buf, sem = refs[-3:]
    step, steps = pl.program_id(0), pl.num_programs(0)
    rows, slots = buf.shape[2:]
    tile = min(rows, 64)
    scale = 2.0 / (reach + 2)

    def band(index):
        low, high = jnp.int32(reach), jnp.int32(reach)
        for s in range(reach):
            low = low - flags_ref[first + index, s]
            high = high + flags_ref[first + index, s + reach + 1]
        return low, high + 1

    def copy(index, s):
        half = lax.rem(index, 2)
        return pltpu.make_async_copy(buf.at[half, s], out_ref.at[index, s], sem.at[half, s])

    def drain(index):
        low, high = band(index)
        lax.fori_loop(low, high, lambda s, carry: (copy(index, s).wait(), carry)[1], 0)

    @pl.when(step >= 2)
    def _():
        drain(step - 2)

    low, high = band(step)

    def part(t, carry):
        at = pl.ds(pl.multiple_of(t * tile, tile), tile)
        node = node_ref[0, at, :] * scale
        node_x = jnp.broadcast_to(node[:, 0:1], (tile, slots))
        node_y = jnp.broadcast_to(node[:, 1:2], (tile, slots))

        def pair(s, inner_carry):
            meta = meta_ref[first + step + s].astype(F32)
            delta_x = ((s - reach).astype(F32) + meta[0:1, :]) * scale - node_x
            delta_y = meta[1:2, :] * scale - node_y
            square = delta_x * delta_x + delta_y * delta_y
            inverse = lax.rsqrt(jnp.maximum(square, 1e-30))
            z = square * inverse
            inner = 1.0 + square * (-5.0 / 3.0 + z * (0.625 + z * (0.5 - 0.25 * z)))
            past = jnp.maximum(z - 1.0, 0.0)
            past_square = past * past
            more = past_square * past_square * past * (1.0 / 3.0 + (2.0 / 3.0) * inverse)
            buf[lax.rem(step, 2), s, at, :] = jnp.where(z < 2.0, inner + more, 0.0)
            return inner_carry

        lax.fori_loop(low, high, pair, 0)
        return carry

    lax.fori_loop(0, rows // tile, part, 0)
    lax.fori_loop(low, high, lambda s, carry: (copy(step, s).start(), carry)[1], 0)

    @pl.when(step == steps - 1)
    def _():
        @pl.when(steps >= 2)
        def _():
            drain(step - 1)

        drain(step)


def tapers(first, here, flags, node_xy, meta, reach, after):
    _, rows, _ = node_xy.shape
    slots = meta.shape[2]
    width = flags.shape[1]
    return pl.pallas_call(
        functools.partial(taper_kernel, reach, first),
        grid=(here,),
        in_specs=[
            pl.BlockSpec(memory_space=pltpu.SMEM),
            pl.BlockSpec((1, rows, 2), lambda d: (first + d, 0, 0)),
            pl.BlockSpec(memory_space=pltpu.VMEM),
            *[WHOLE] * len(after),
        ],
        out_specs=WHOLE,
        out_shape=jax.ShapeDtypeStruct((here, width, rows, slots), F32),
        scratch_shapes=[
            pltpu.VMEM((2, width, rows, slots), F32),
            pltpu.SemaphoreType.DMA((2, width)),
        ],
        compiler_params=params(),
        cost_estimate=cost(3 * here),
        name="taper",
    )(flags, node_xy, meta, *after)


def spread_row(obs, meta, degrees):
    slots, members = obs.shape
    lanes = min(members, 128)
    total = jnp.zeros((slots, lanes), F32)
    for j in range(members // lanes):
        block = obs[:, j * lanes : (j + 1) * lanes].astype(F32)
        total = total + block * block
    ones = jnp.ones((8, lanes), BF)
    row = jnp.zeros((8, slots), F32)
    for _ in range(3):
        part = total.astype(BF)
        total = total - part.astype(F32)
        row = row + lax.dot_general(
            ones, part, (((1,), (1,)), ((), ())), preferred_element_type=F32
        )
    return meta[3:4, :].astype(F32) / (row[0:1, :] + degrees * meta[2:3, :].astype(F32))


def own_spread_kernel(reach, degrees, obs_ref, meta_ref, *refs):
    out_ref = refs[-1]
    for d in range(obs_ref.shape[0]):
        out_ref[d] = spread_row(obs_ref[d], meta_ref[reach + d], degrees)


def own_spread(obs, meta, reach, after):
    count, slots, members = obs.shape
    vmem = pl.BlockSpec(memory_space=pltpu.VMEM)
    return pl.pallas_call(
        functools.partial(own_spread_kernel, reach, float(members - 1)),
        in_specs=[vmem, vmem, *[WHOLE] * len(after)],
        out_specs=vmem,
        out_shape=jax.ShapeDtypeStruct((count, 1, slots), F32),
        compiler_params=params(),
        cost_estimate=cost(SPREAD_COST),
        name="own_spread",
    )(obs, meta, *after)


def all_spread_kernel(degrees, before_ref, after_ref, own_ref, meta_ref, out_ref):
    reach, count = before_ref.shape[1], own_ref.shape[0]
    out_ref[reach : reach + count] = own_ref[...]
    for d in range(reach):
        out_ref[d] = spread_row(before_ref[0, d], meta_ref[d], degrees)
        e = reach + count + d
        out_ref[e] = spread_row(after_ref[0, d], meta_ref[e], degrees)


def all_spread(edges, own, meta):
    _, reach, slots, members = edges[0].shape
    edge = pl.BlockSpec((1, reach, slots, members), lambda i: (1, 0, 0, 0))
    return pl.pallas_call(
        functools.partial(all_spread_kernel, float(members - 1)),
        grid=(1,),
        in_specs=[
            edge,
            edge,
            pl.BlockSpec(own.shape, lambda i: (0, 0, 0)),
            pl.BlockSpec(meta.shape, lambda i: (0, 0, 0)),
        ],
        out_specs=pl.BlockSpec((meta.shape[0], 1, slots), lambda i: (0, 0, 0)),
        out_shape=jax.ShapeDtypeStruct((meta.shape[0], 1, slots), F32),
        compiler_params=params(),
        cost_estimate=cost(4),
        name="all_spread",
    )(*edges, own, meta)


def pair_kernel(first, reach, here, parts, routes, bases, *refs):
    flags_ref, taper_ref, scale_ref, table_ref = refs[:4]
    before_ref, after_ref, obs_ref, innov_ref = refs[4:8]
    obs_refs = (before_ref.at[1], obs_ref, after_ref.at[1])
    innov_refs = (before_ref.at[0], innov_ref, after_ref.at[0])
    piece_refs = refs[8 : 8 + len(bases)]
    out_ref, x_buf, t_buf, obs_buf, innov_buf, total, x_sem, sem, out_sem = refs[-9:]
    rows, width = table_ref.shape[1] // parts, table_ref.shape[2]
    own, slots = obs_ref.shape[:2]
    me = lax.axis_index("mem")

    def band(index):
        low, high = jnp.int32(reach), jnp.int32(reach)
        for s in range(reach):
            low = low - flags_ref[first + index, s]
            high = high + flags_ref[first + index, s + reach + 1]
        return low, high + 1

    def x_copy(index, j, block):
        half = lax.rem(index, 2)
        return pltpu.make_async_copy(
            block, x_buf.at[half, :, j * width : (j + 1) * width], x_sem.at[half, j]
        )

    def x_start(index, j):
        @pl.when(me == j)
        def _():
            x_copy(index, j, table_ref.at[first + index, j * rows : (j + 1) * rows, :]).start()

        for r, base in enumerate(bases):
            takers = [z for z in range(parts) if routes.get((z, j)) == r]
            if takers:
                wanted = functools.reduce(jnp.logical_or, [me == z for z in takers])

                @pl.when(wanted)
                def _(r=r, base=base):
                    if len(piece_refs[r].shape) == 4:
                        block = piece_refs[r].at[j, first - base + index]
                    else:
                        at = pl.multiple_of((first - base + index) * rows, rows)
                        block = piece_refs[r].at[pl.ds(at, rows)]
                    x_copy(index, j, block).start()

    def t_copy(index, s):
        half = lax.rem(index, 2)
        return pltpu.make_async_copy(
            taper_ref.at[index, s], t_buf.at[half, s], sem.at[half, s, 0]
        )

    def row_copies(index, s, part, at):
        half = lax.rem(index, 2)
        here_rows = pl.ds(pl.multiple_of(s * slots, slots), slots)
        return (
            pltpu.make_async_copy(
                obs_refs[part].at[at], obs_buf.at[half, here_rows], sem.at[half, s, 1]
            ),
            pltpu.make_async_copy(
                innov_refs[part].at[at], innov_buf.at[half, here_rows], sem.at[half, s, 2]
            ),
        )

    def out_copy(index):
        half = lax.rem(index, 2)
        return pltpu.make_async_copy(total.at[half], out_ref.at[first + index], out_sem.at[half])

    def fetch(index):
        for j in range(parts):
            x_start(index, j)
        low, high = band(index)

        def one(s, carry):
            t_copy(index, s).start()
            at = first + index + s - reach

            @pl.when(at < 0)
            def _():
                for copy in row_copies(index, s, 0, at + reach):
                    copy.start()

            @pl.when(jnp.logical_and(at >= 0, at < own))
            def _():
                for copy in row_copies(index, s, 1, at):
                    copy.start()

            @pl.when(at >= own)
            def _():
                for copy in row_copies(index, s, 2, at - own):
                    copy.start()

            return carry

        lax.fori_loop(low, high, one, 0)

    def district(index, carry):
        half = lax.rem(index, 2)

        @pl.when(index + 1 < here)
        def _():
            fetch(index + 1)

        @pl.when(index >= 2)
        def _():
            out_copy(index - 2).wait()

        for j in range(parts):
            x_copy(index, j, table_ref.at[0, 0:rows, :]).wait()
        low, high = band(index)
        odd = lax.rem(high - low, 2)

        def step(s, taken):
            for j in range(taken):
                t_copy(index, s + j).wait()
                for copy in row_copies(index, s + j, 1, 0):
                    copy.wait()
            at = pl.ds(pl.multiple_of(s * slots, slots), taken * slots)
            cov = lax.dot_general(
                x_buf[half], obs_buf[half, at], (((1,), (1,)), ((), ())), preferred_element_type=F32
            )
            gains = [
                (
                    t_buf[half, s + j]
                    * (cov[:, j * slots : (j + 1) * slots] * scale_ref[first + index + s + j])
                ).astype(BF)
                for j in range(taken)
            ]
            gain = gains[0] if taken == 1 else jnp.concatenate(gains, axis=1)
            return jnp.dot(gain, innov_buf[half, at], preferred_element_type=F32)

        @pl.when(odd == 1)
        def _():
            total[half] = step(low, 1)

        @pl.when(odd == 0)
        def _():
            total[half] = step(low, 2)

        def two(i, inner_carry):
            total[half] += step(low + 2 - odd + 2 * i, 2)
            return inner_carry

        lax.fori_loop(0, (high - low - 2 + odd) // 2, two, 0)
        out_copy(index).start()
        return carry

    fetch(0)
    lax.fori_loop(0, here, district, 0)
    for index in range(max(here - 2, 0), here):
        out_copy(index).wait()


def pairs(first, flags, taper, scale, table, pieces, routes, edges, obs, innov, out):
    count = table.shape[0]
    here, _, rows, _ = taper.shape
    parts = table.shape[1] // rows
    bases = [base for _, base in pieces]
    slots, members = obs.shape[1:]
    slot_count = flags.shape[1]
    reach = (slot_count - 1) // 2
    operands = [flags, taper, scale, table, *edges, obs, innov, *[array for array, _ in pieces]]
    in_specs = [
        pl.BlockSpec(memory_space=pltpu.SMEM),
        WHOLE,
        pl.BlockSpec(memory_space=pltpu.VMEM),
        *[WHOLE] * (5 + len(pieces)),
    ]
    aliases = {}
    if out is not None:
        aliases = {len(operands): 0}
        operands.append(out)
        in_specs.append(WHOLE)
    return pl.pallas_call(
        functools.partial(pair_kernel, first, reach, here, parts, routes, bases),
        in_specs=in_specs,
        out_specs=WHOLE,
        out_shape=jax.ShapeDtypeStruct((count, rows, members), F32),
        scratch_shapes=[
            pltpu.VMEM((2, rows, members), BF),
            pltpu.VMEM((2, slot_count, rows, slots), F32),
            pltpu.VMEM((2, slot_count * slots, members), BF),
            pltpu.VMEM((2, slot_count * slots, members), BF),
            pltpu.VMEM((2, rows, members), F32),
            pltpu.SemaphoreType.DMA((2, parts)),
            pltpu.SemaphoreType.DMA((2, slot_count, 3)),
            pltpu.SemaphoreType.DMA((2,)),
        ],
        input_output_aliases=aliases,
        compiler_params=params(),
        cost_estimate=cost(3 * here),
        name="pairs",
    )(*operands)


def move(copies):
    for load, _ in copies:
        load.start()
    for load, store in copies:
        load.wait()
        store.start()
    for _, store in copies:
        store.wait()


def mover(kernel, shape, buffer, operands, name):
    return pl.pallas_call(
        kernel,
        in_specs=[WHOLE] * len(operands),
        out_specs=WHOLE,
        out_shape=jax.ShapeDtypeStruct(shape, BF),
        scratch_shapes=[
            pltpu.VMEM(buffer, BF),
            pltpu.SemaphoreType.DMA((2, *buffer[:-2])),
        ],
        compiler_params=params(),
        cost_estimate=cost(2),
        name=name,
    )(*operands)


def cut_kernel(start, targets, extra, *refs):
    table_ref = refs[0]
    out_ref, buf, sem = refs[-3:]
    parts = len(targets)
    rows = table_ref.shape[1] // parts
    size = (out_ref.shape[0] - extra) // rows
    me = lax.axis_index("mem")

    def run(target):
        copies = []
        for i in range(size):
            src = table_ref.at[start + i, target * rows : (target + 1) * rows, :]
            copies.append((src, slice(i * rows, (i + 1) * rows)))
        for i in range(refs[1].shape[0] if extra else 0):
            slots = refs[1].shape[1]
            first = size * rows + i * slots
            copies.append((refs[1].at[i], slice(first, first + slots)))
        move([
            (
                pltpu.make_async_copy(src, buf.at[to], sem.at[0, n]),
                pltpu.make_async_copy(buf.at[to], out_ref.at[to], sem.at[1, n]),
            )
            for n, (src, to) in enumerate(copies)
        ])

    for target in sorted(set(targets)):
        senders = [z for z in range(parts) if targets[z] == target]
        here = functools.reduce(jnp.logical_or, [me == z for z in senders])

        @pl.when(here)
        def _(target=target):
            run(target)


def cut(table, start, size, targets, extra, after, length=2):
    rows, width = table.shape[1] // len(targets), table.shape[2]
    blocks = (table,) if extra is None else (table, extra)
    more = 0 if extra is None else extra.shape[0] * extra.shape[1]
    shape = (size * rows + more, width)
    operands = (*blocks, *after)
    return pl.pallas_call(
        functools.partial(cut_kernel, start, targets, more),
        in_specs=[WHOLE] * len(operands),
        out_specs=WHOLE,
        out_shape=jax.ShapeDtypeStruct(shape, BF),
        scratch_shapes=[
            pltpu.VMEM(shape, BF),
            pltpu.SemaphoreType.DMA((2, size + (0 if extra is None else extra.shape[0]))),
        ],
        compiler_params=params(),
        cost_estimate=cost(length),
        name="cut",
    )(*operands)


def cut_all_kernel(start, *refs):
    table_ref = refs[0]
    out_ref, buf, sem = refs[-3:]
    parts, size = out_ref.shape[0], out_ref.shape[1]
    rows = out_ref.shape[2]
    move([
        (
            pltpu.make_async_copy(
                table_ref.at[start + i, j * rows : (j + 1) * rows, :], buf.at[j, i], sem.at[0, j, i]
            ),
            pltpu.make_async_copy(buf.at[j, i], out_ref.at[j, i], sem.at[1, j, i]),
        )
        for j in range(parts)
        for i in range(size)
    ])


def cut_all(table, start, size, parts, after):
    shape = (parts, size, table.shape[1] // parts, table.shape[2])
    return mover(functools.partial(cut_all_kernel, start), shape, shape, (table, *after), "cut_all")


def slots_of(ref, i, count, slots):
    if len(ref.shape) == 3:
        return ref.at[i]
    first = ref.shape[0] - (count - i) * slots
    return ref.at[first : first + slots]


def relay_kernel(*refs):
    p1, p2, p3 = refs[:3]
    out_ref, buf, sem = refs[-3:]
    me = lax.axis_index("mem")
    count, slots, _ = p3.shape

    def run(p4):
        move([
            (
                pltpu.make_async_copy(
                    slots_of(src, i, count, slots), buf.at[k, i], sem.at[0, k, i]
                ),
                pltpu.make_async_copy(buf.at[k, i], out_ref.at[k, i], sem.at[1, k, i]),
            )
            for k, src in enumerate((p4, p3))
            for i in range(count)
        ])

    @pl.when(me == 2)
    def _():
        run(p1)

    @pl.when(me != 2)
    def _():
        run(p2)


def relay(p1, p2, p3, after):
    shape = (2, *p3.shape)
    return mover(relay_kernel, shape, shape, (p1, p2, p3, *after), "relay")


def place_kernel(edges, *refs):
    own, p1, p2, p3, far = refs[:5]
    me = lax.axis_index("mem")
    count, slots, width = own.shape
    if edges:
        other = refs[5]
        out_ref, last_ref, first_ref, buf, edge, sem, edge_sem = refs[-7:]
        sides = [(first_ref, 0), (last_ref, count - edges)]
        for n, (_, at) in enumerate(sides):
            pltpu.make_async_copy(
                other.at[at : at + edges], edge.at[n], edge_sem.at[0, n]
            ).start()
    else:
        out_ref, buf, sem = refs[-3:]
        sides = []
    p4, p5 = far.at[0], far.at[1]
    table = (
        (own, p2, p4, p5),
        (p1, own, p2, p3),
        (p3, p1, own, p2),
        (p5, p4, p1, own),
    )
    order = list(range(count))
    for z, sources in enumerate(table):

        @pl.when(me == z)
        def _(sources=sources):
            copies = []
            for i in order:
                for j, src in enumerate(sources):
                    copies.append((
                        pltpu.make_async_copy(
                            slots_of(src, i, count, slots), buf.at[j, i], sem.at[0, j, i]
                        ),
                        pltpu.make_async_copy(
                            buf.at[j, i],
                            out_ref.at[i, :, j * width : (j + 1) * width],
                            sem.at[1, j, i],
                        ),
                    ))
            move(copies)

    copies = []
    for n, (side_ref, at) in enumerate(sides):
        pltpu.make_async_copy(other.at[at : at + edges], edge.at[n], edge_sem.at[0, n]).wait()
        copies.append(pltpu.make_async_copy(edge.at[n], side_ref.at[0], edge_sem.at[1, n]))
        for d in range(edges):
            for j in range(4):
                copies.append(
                    pltpu.make_async_copy(
                        buf.at[j, at + d],
                        side_ref.at[1, d, :, j * width : (j + 1) * width],
                        sem.at[n, j, d],
                    )
                )
    for copy in copies:
        copy.start()
    for copy in copies:
        copy.wait()


def place(own, near, far, edges, after):
    count, slots, width = own.shape
    operands = (own, *near, far, *after)
    shapes = [jax.ShapeDtypeStruct((count, slots, 4 * width), BF)]
    scratch = [pltpu.VMEM((4, count, slots, width), BF)]
    sems = [pltpu.SemaphoreType.DMA((2, 4, count))]
    if edges:
        shapes += [jax.ShapeDtypeStruct((2, edges, slots, 4 * width), BF)] * 2
        scratch.append(pltpu.VMEM((2, edges, slots, 4 * width), BF))
        sems.append(pltpu.SemaphoreType.DMA((2, 2)))
    return pl.pallas_call(
        functools.partial(place_kernel, edges),
        in_specs=[WHOLE] * len(operands),
        out_specs=[WHOLE] * len(shapes),
        out_shape=shapes,
        scratch_shapes=scratch + sems,
        compiler_params=params(),
        cost_estimate=cost(0.1 if edges else 3),
        name="place",
    )(*operands)


def pass_kernel(*refs):
    refs[-1][...] = refs[0][...]


def passed(array, after):
    vmem = pl.BlockSpec(memory_space=pltpu.VMEM)
    return pl.pallas_call(
        pass_kernel,
        in_specs=[vmem] + [WHOLE] * len(after),
        out_specs=vmem,
        out_shape=jax.ShapeDtypeStruct(array.shape, array.dtype),
        compiler_params=params(),
        cost_estimate=cost(0.1),
        name="passed",
    )(array, *after)


UP = ((0, 1), (1, 2), (2, 3))
DOWN = ((1, 0), (2, 1), (3, 2))


def hop(block, pairs_of):
    return lax.ppermute(block, "mem", pairs_of)


def last_hop(block):
    return lax.ppermute(block, "mem", [(2, 3), (1, 0)])


def shifts():
    devices = lax.axis_size("dist")
    up = [(i, i + 1) for i in range(devices - 1)]
    return up, [(j, i) for i, j in up]


def halo(last, first):
    up, down = shifts()
    return lax.ppermute(last, "dist", up), lax.ppermute(first, "dist", down)


def on_device(anomalies, innovations, obs_var, node_pos, obs_node, obs_count, in_radius):
    count, nodes, width = anomalies.shape
    slots = obs_node.shape[1]
    reach = (in_radius.shape[1] - 1) // 2
    parts = lax.axis_size("mem")
    me = lax.axis_index("mem")
    rows = nodes // parts
    chunks = CHUNKS if sum(CHUNKS) == count else (1,) * count
    starts = [sum(chunks[:c]) for c in range(len(chunks))]
    last = len(chunks) - 1
    taper = {}

    def weigh(c, *after):
        taper[c] = tapers(starts[c], chunks[c], in_radius, node_xy, ext_meta, reach, after)
        return taper[c]

    pos = jnp.transpose(node_pos, (1, 0, 2))
    observed, obs_xy = pick(anomalies, obs_node, pos, ())
    live = jnp.arange(slots, dtype=jnp.int32)[None, :] < obs_count[:, None]
    meta = jnp.concatenate([obs_xy, obs_var[:, None, :], live[:, None, :].astype(BF)], axis=1)
    node_xy = lax.dynamic_slice_in_dim(node_pos, me * rows, rows, 2)
    node_xy = jnp.transpose(node_xy, (1, 2, 0)).astype(F32)

    if parts == 4:
        far_pairs = ((0, 2), (3, 1))
        above, below, through = (1, 2, 3, 3), (0, 0, 1, 2), (3, 3, 0, 0)
        near_innov = (
            hop(innovations, UP), hop(innovations, DOWN), hop(innovations, far_pairs)
        )
        up = hop(cut(anomalies, 0, count, above, None, ()), UP)
        down = hop(cut(anomalies, 0, count, below, None, ()), DOWN)
        near_obs = (hop(observed, UP), hop(observed, DOWN), hop(observed, far_pairs))
        relay_innov = relay(*near_innov, ())
        far_innov = last_hop(relay_innov)
        meta = passed(meta, (relay_innov,))
        meta_before, meta_after = halo(meta[-reach:], meta[:reach])
        ext_meta = jnp.concatenate([meta_before, meta, meta_after], axis=0)
        weigh(0, relay_innov, up, down)
        relay_obs = relay(*near_obs, (taper[0],))
        far_obs = last_hop(relay_obs)
        middle = hop(cut(anomalies, 0, count, (2, 2, 1, 1), None, (relay_obs,)), far_pairs)
        (full_innov,) = place(innovations, near_innov, far_innov, 0, (relay_obs,))
        weigh(1, full_innov)
        full_obs, last, first = place(
            observed, near_obs, far_obs, reach, (full_innov, taper[1], middle)
        )
        edges = halo(last, first)
        end_block = cut(anomalies, 0, count, through, None, (full_obs,), 0.1)
        ends = hop(end_block, ((0, 3), (3, 0)))
        cross = [
            hop(cut(anomalies, start, here, through, None, (full_obs,), 0.1), ((1, 3), (2, 0)))
            for start, here in zip(starts, chunks)
        ]
        own_scale = own_spread(full_obs, ext_meta, reach, (ends,))
        pieces = [
            [(up, 0), (down, 0), (middle, 0), (ends, 0), (block, start)]
            for block, start in zip(cross, starts)
        ]
        routes = {
            (1, 0): 0, (2, 1): 0, (3, 2): 0,
            (0, 1): 1, (1, 2): 1, (2, 3): 1,
            (2, 0): 2, (1, 3): 2,
            (3, 0): 3, (0, 3): 3,
            (3, 1): 4, (0, 2): 4,
        }
    else:
        meta_before, meta_after = halo(meta[-reach:], meta[:reach])
        ext_meta = jnp.concatenate([meta_before, meta, meta_after], axis=0)
        full_innov = lax.all_gather(innovations, "mem", axis=2, tiled=True)
        full_obs = lax.all_gather(observed, "mem", axis=2, tiled=True)
        both = jnp.stack([full_innov, full_obs])
        edges = halo(both[:, -reach:], both[:, :reach])
        pieces = []
        for c, (first, size) in enumerate(zip(starts, chunks)):
            weigh(c)
            order = ()
            turns = [[(i, (i + k) % parts) for i in range(parts)] for k in range(1, parts)]
            pieces.append([
                (
                    hop(
                        cut(anomalies, first, size, tuple(t for _, t in turn), None, ()), turn
                    ),
                    first,
                )
                for turn in turns
            ])
        routes = {
            (z, j): (z - j) % parts - 1 for z in range(parts) for j in range(parts) if z != j
        }
    if parts != 4:
        own_scale = own_spread(full_obs, ext_meta, reach, ())
    scale = all_spread(edges, own_scale, ext_meta)

    out = None
    for c in range(len(chunks)):
        out = pairs(
            starts[c],
            in_radius,
            taper[c],
            scale,
            anomalies,
            pieces[c],
            routes,
            edges,
            full_obs,
            full_innov,
            out,
        )
    return out


def solution(mesh):
    return jax.shard_map(
        on_device,
        mesh=mesh,
        in_specs=(
            P("dist", None, "mem"),
            P("dist", None, "mem"),
            P("dist", None),
            P(None, "dist", None),
            P("dist", None),
            P("dist"),
            P("dist", None),
        ),
        out_specs=P("dist", "mem", None),
        check_vma=False,
    )
```

profile of v0, /device:TPU:1, one launch (start us, length us, event | category | flops | bytes accessed | tf_op | source)
XLA Modules:
  0.0 187.6 jit_solution(1926760876103283783)
XLA Ops:
  0.0 4.8 %collective-permute-start = (bf16[8,256,128]{2,1,0:T(8,128)(2,1)}, bf16[8,256,128]{2,1,0:T(8,128)(2,1)}, u32[]{:S(2)}, u32[]{:S(2)}) collective-permute-start(bf16[8,256,128]{2,1,0:T(8,128)(2,1)} %refs_0_.14), channel_id=1, source_target_pairs={{0,1},{1,2},{2,3},{4,5},{5,6},{6,7},{8,9},{9,10},{10,11},{12,13},{... | collective-permute-start | bytes 1572872 | tf_op jit(solution)/shard_map/ppermute | solution.py:659
  6.1 5.1 %collective-permute-start.2 = (bf16[8,256,128]{2,1,0:T(8,128)(2,1)}, bf16[8,256,128]{2,1,0:T(8,128)(2,1)}, u32[]{:S(2)}, u32[]{:S(2)}) collective-permute-start(bf16[8,256,128]{2,1,0:T(8,128)(2,1)} %refs_0_.14), channel_id=1, source_target_pairs={{0,2},{3,1},{4,6},{7,5},{8,10},{11,9},{12,14},{15,13},{16,18},{19,... | collective-permute-start | bytes 1572872 | tf_op jit(solution)/shard_map/ppermute | solution.py:659
  11.2 2.1 %cut.7 = bf16[4096,128]{1,0:T(8,128)(2,1)} custom-call(bf16[8,2048,128]{2,1,0:T(8,128)(2,1)} %refs_3_.3), custom_call_target="tpu_custom_call" | custom-call | flops 2302560000 | bytes 7380000 | tf_op jit(solution)/shard_map/cut/pallas_call | solution.py:478
  14.7 2.1 %cut.6 = bf16[4096,128]{1,0:T(8,128)(2,1)} custom-call(bf16[8,2048,128]{2,1,0:T(8,128)(2,1)} %refs_3_.3), custom_call_target="tpu_custom_call" | custom-call | flops 2302560000 | bytes 7380000 | tf_op jit(solution)/shard_map/cut/pallas_call | solution.py:478
  16.8 5.0 %collective-permute-start.9 = (bf16[4096,128]{1,0:T(8,128)(2,1)}, bf16[4096,128]{1,0:T(8,128)(2,1)}, u32[]{:S(2)}, u32[]{:S(2)}) collective-permute-start(bf16[4096,128]{1,0:T(8,128)(2,1)} %cut.6), channel_id=1, source_target_pairs={{0,1},{1,2},{2,3},{4,5},{5,6},{6,7},{8,9},{9,10},{10,11},{12,13},{... | collective-permute-start | bytes 3145736 | tf_op jit(solution)/shard_map/ppermute | solution.py:659
  23.9 8.8 %pick.1 = (bf16[8,256,128]{2,1,0:T(8,128)(2,1)}, bf16[8,2,256]{2,1,0:T(2,128)(2,1)}) custom-call(s32[8,256,1]{2,1,0:T(8,128)} %copy.13.node_ref, bf16[8,2048,128]{2,1,0:T(8,128)(2,1)} %refs_3_.3, bf16[8,2,2048]{2,1,0:T(2,128)(2,1)} %bitcast.7), custom_call_target="tpu_custom_call" | custom-call | flops 8058959872 | bytes 25830000 | tf_op jit(solution)/shard_map/pick/pallas_call | solution.py:41
  36.0 2.3 %relay.2.refs_1_.refs_3_ = bf16[2,8,256,128]{3,2,1,0:T(8,128)(2,1)} custom-call(bf16[8,256,128]{2,1,0:T(8,128)(2,1)} %collective-permute-done.refs_0_.refs_1_, bf16[8,256,128]{2,1,0:T(8,128)(2,1)} %collective-permute-done.1.refs_1_.refs_2_, bf16[8,256,128]{2,1,0:T(8,128)(2,1)} %collective-permute-done.2.refs_2_.refs_3_), custom_call_target="tpu_custom_call" | custom-call | flops 2302560000 | bytes 7380000 | tf_op jit(solution)/shard_map/relay/pallas_call | solution.py:423
  40.4 5.1 %collective-permute-start.3 = (bf16[3,4,256]{2,1,0:T(4,128)(2,1)S(1)}, bf16[3,4,256]{2,1,0:T(4,128)(2,1)S(1)}, u32[]{:S(2)}, u32[]{:S(2)}) collective-permute-start(bf16[3,4,256]{2,1,0:T(4,128)(2,1)S(1)} %get-tuple-element.15), channel_id=1, source_target_pairs={{0,4},{4,8},{8,12},{12,16},{16,20},{20,24},{24,28},{1,5},{5,9},{9,... | collective-permute-start | bytes 18440 | tf_op jit(solution)/shard_map/ppermute | solution.py:674
  45.4 1.9 %collective-permute-start.4 = (bf16[3,4,256]{2,1,0:T(4,128)(2,1)S(1)}, bf16[3,4,256]{2,1,0:T(4,128)(2,1)S(1)}, u32[]{:S(2)}, u32[]{:S(2)}) collective-permute-start(bf16[3,4,256]{2,1,0:T(4,128)(2,1)S(1)} %get-tuple-element.16), channel_id=1, source_target_pairs={{4,0},{8,4},{12,8},{16,12},{20,16},{24,20},{28,24},{5,1},{9,5},{13... | collective-permute-start | bytes 18440 | tf_op jit(solution)/shard_map/ppermute | solution.py:674
  47.4 1.5 convert_bitcast_fusion.refs_1_
  50.4 4.3 %collective-permute-start.8 = (bf16[8,256,128]{2,1,0:T(8,128)(2,1)}, bf16[8,256,128]{2,1,0:T(8,128)(2,1)S(1)}, u32[]{:S(2)}, u32[]{:S(2)}) collective-permute-start(bf16[8,256,128]{2,1,0:T(8,128)(2,1)} %get-tuple-element.11.refs_0_), channel_id=1, source_target_pairs={{0,2},{3,1},{4,6},{7,5},{8,10},{11,9},{12,14},{15,13},{16,18},{19,... | collective-permute-start | bytes 1572872 | tf_op jit(solution)/shard_map/ppermute | solution.py:659
  56.6 10.9 %taper.2.refs_3_.refs_1_ = f32[5,7,512,256]{3,2,1,0:T(8,128)} custom-call(s32[8,7]{1,0:T(8,128)} %refs_0_.21, f32[8,512,2]{2,1,0:T(8,128)} %convert_bitcast_fusion.refs_1_, bf16[14,4,256]{2,1,0:T(4,128)(2,1)} %pad_maximum_fusion.refs_2_.meta_ref, bf16[2,8,256,128]{3,2,1,0:T(8,128)(2,1)} %relay.2.refs_1_.refs_3_, ...), custom_call_target="tpu_custom_call" | custom-call | flops 17269200896 | bytes 55350000 | tf_op jit(solution)/shard_map/taper/pallas_call | solution.py:132
  67.6 3.5 %collective-permute-done.8.refs_2_.refs_3_ = bf16[8,256,128]{2,1,0:T(8,128)(2,1)S(1)} collective-permute-done((bf16[8,256,128]{2,1,0:T(8,128)(2,1)}, bf16[8,256,128]{2,1,0:T(8,128)(2,1)S(1)}, u32[]{:S(2)}, u32[]{:S(2)}) %collective-permute-start.8) | collective-permute-done | bytes 524320 | tf_op jit(solution)/shard_map/ppermute | solution.py:659
  72.0 2.2 %relay.3.refs_5_.refs_1_ = bf16[2,8,256,128]{3,2,1,0:T(8,128)(2,1)} custom-call(bf16[8,256,128]{2,1,0:T(8,128)(2,1)} %copy-done.1, bf16[8,256,128]{2,1,0:T(8,128)(2,1)} %copy-done.2, bf16[8,256,128]{2,1,0:T(8,128)(2,1)} %copy-done.3, f32[5,7,512,256]{3,2,1,0:T(8,128)} %taper.2.refs_3_.refs_1_), custom_call_target="tpu_custom_call" | custom-call | flops 2302560000 | bytes 7380000 | tf_op jit(solution)/shard_map/relay/pallas_call | solution.py:423
  75.5 2.1 %cut.8 = bf16[4096,128]{1,0:T(8,128)(2,1)} custom-call(bf16[8,2048,128]{2,1,0:T(8,128)(2,1)} %refs_3_.3, bf16[2,8,256,128]{3,2,1,0:T(8,128)(2,1)} %relay.3.refs_5_.refs_1_), custom_call_target="tpu_custom_call" | custom-call | flops 2302560000 | bytes 7380000 | tf_op jit(solution)/shard_map/cut/pallas_call | solution.py:478
  77.6 8.9 %collective-permute-start.12 = (bf16[4096,128]{1,0:T(8,128)(2,1)}, bf16[4096,128]{1,0:T(8,128)(2,1)S(1)}, u32[]{:S(2)}, u32[]{:S(2)}) collective-permute-start(bf16[4096,128]{1,0:T(8,128)(2,1)} %cut.8), channel_id=1, source_target_pairs={{0,2},{3,1},{4,6},{7,5},{8,10},{11,9},{12,14},{15,13},{16,18},{19,... | collective-permute-start | bytes 3145736 | tf_op jit(solution)/shard_map/ppermute | solution.py:659
  86.5 2.8 %place.2.refs_3_.refs_5_.refs_7_ = bf16[8,256,512]{2,1,0:T(8,128)(2,1)} custom-call(bf16[8,256,128]{2,1,0:T(8,128)(2,1)} %refs_0_.14, bf16[8,256,128]{2,1,0:T(8,128)(2,1)} %collective-permute-done.refs_0_.refs_1_, bf16[8,256,128]{2,1,0:T(8,128)(2,1)} %collective-permute-done.1.refs_1_.refs_2_, bf16[8,256,128]{2,1,0:T(8,128)(2,1)} %collective-permute-done.2.refs_2_.refs_3_, ...), custom_call_target="tpu_custom_call" | custom-call | flops 3453839872 | bytes 11070000 | tf_op jit(solution)/shard_map/place/pallas_call | solution.py:625
  89.3 10.3 %taper.3.refs_6_.refs_1_ = f32[3,7,512,256]{3,2,1,0:T(8,128)} custom-call(s32[8,7]{1,0:T(8,128)} %refs_0_.21, f32[8,512,2]{2,1,0:T(8,128)} %convert_bitcast_fusion.refs_1_, bf16[14,4,256]{2,1,0:T(4,128)(2,1)} %pad_maximum_fusion.refs_2_.meta_ref, bf16[8,256,512]{2,1,0:T(8,128)(2,1)} %place.2.refs_3_.refs_5_.refs_7_), custom_call_target="tpu_custom_call" | custom-call | flops 10361520128 | bytes 33210000 | tf_op jit(solution)/shard_map/taper/pallas_call | solution.py:132
  99.6 7.4 %collective-permute-done.12.refs_7_.refs_10_ = bf16[4096,128]{1,0:T(8,128)(2,1)S(1)} collective-permute-done((bf16[4096,128]{1,0:T(8,128)(2,1)}, bf16[4096,128]{1,0:T(8,128)(2,1)S(1)}, u32[]{:S(2)}, u32[]{:S(2)}) %collective-permute-start.12) | collective-permute-done | bytes 1048608 | tf_op jit(solution)/shard_map/ppermute | solution.py:659
  108.0 4.9 %place.3 = (bf16[8,256,512]{2,1,0:T(8,128)(2,1)}, bf16[2,3,256,512]{3,2,1,0:T(8,128)(2,1)}, bf16[2,3,256,512]{3,2,1,0:T(8,128)(2,1)}) custom-call(bf16[8,256,128]{2,1,0:T(8,128)(2,1)} %get-tuple-element.11.refs_0_, bf16[8,256,128]{2,1,0:T(8,128)(2,1)} %copy-done.1, bf16[8,256,128]{2,1,0:T(8,128)(2,1)} %copy-done.2, bf16[8,256,128]{2,1,0:T(8,128)(2,1)} %copy-done.3, ...), custom_call_target="tpu_custom_call" | custom-call | flops 115128000 | bytes 369000 | tf_op jit(solution)/shard_map/place/pallas_call | solution.py:625
  112.9 2.1 %cut.9 = bf16[4096,128]{1,0:T(8,128)(2,1)} custom-call(bf16[8,2048,128]{2,1,0:T(8,128)(2,1)} %refs_3_.3, bf16[8,256,512]{2,1,0:T(8,128)(2,1)} %get-tuple-element.14.refs_1_.obs_ref.refs_6_), custom_call_target="tpu_custom_call" | custom-call | flops 115128000 | bytes 369000 | tf_op jit(solution)/shard_map/cut/pallas_call | solution.py:478
  115.0 4.3 %collective-permute-start.15 = (bf16[4096,128]{1,0:T(8,128)(2,1)}, bf16[4096,128]{1,0:T(8,128)(2,1)}, u32[]{:S(2)}, u32[]{:S(2)}) collective-permute-start(bf16[4096,128]{1,0:T(8,128)(2,1)} %cut.9), channel_id=1, source_target_pairs={{0,3},{3,0},{4,7},{7,4},{8,11},{11,8},{12,15},{15,12},{16,19},{19,... | collective-permute-start | bytes 3145736 | tf_op jit(solution)/shard_map/ppermute | solution.py:659
  119.3 6.1 %collective-permute-start.13 = (bf16[2,3,256,512]{3,2,1,0:T(8,128)(2,1)}, bf16[2,3,256,512]{3,2,1,0:T(8,128)(2,1)S(1)}, u32[]{:S(2)}, u32[]{:S(2)}) collective-permute-start(bf16[2,3,256,512]{3,2,1,0:T(8,128)(2,1)} %get-tuple-element.12), channel_id=1, source_target_pairs={{0,4},{4,8},{8,12},{12,16},{16,20},{20,24},{24,28},{1,5},{5,9},{9,... | collective-permute-start | bytes 4718600 | tf_op jit(solution)/shard_map/ppermute | solution.py:674
  125.4 1.9 %collective-permute-start.14 = (bf16[2,3,256,512]{3,2,1,0:T(8,128)(2,1)}, bf16[2,3,256,512]{3,2,1,0:T(8,128)(2,1)}, u32[]{:S(2)}, u32[]{:S(2)}) collective-permute-start(bf16[2,3,256,512]{3,2,1,0:T(8,128)(2,1)} %get-tuple-element.13), channel_id=1, source_target_pairs={{4,0},{8,4},{12,8},{16,12},{20,16},{24,20},{28,24},{5,1},{9,5},{13... | collective-permute-start | bytes 4718600 | tf_op jit(solution)/shard_map/ppermute | solution.py:674
  127.3 1.9 %cut.11 = bf16[2560,128]{1,0:T(8,128)(2,1)} custom-call(bf16[8,2048,128]{2,1,0:T(8,128)(2,1)} %refs_3_.3, bf16[8,256,512]{2,1,0:T(8,128)(2,1)} %get-tuple-element.14.refs_1_.obs_ref.refs_6_), custom_call_target="tpu_custom_call" | custom-call | flops 115128000 | bytes 369000 | tf_op jit(solution)/shard_map/cut/pallas_call | solution.py:478
  130.6 1.7 cut.10
  133.6 7.1 %collective-permute-done.15.refs_0_.refs_11_ = bf16[4096,128]{1,0:T(8,128)(2,1)} collective-permute-done((bf16[4096,128]{1,0:T(8,128)(2,1)}, bf16[4096,128]{1,0:T(8,128)(2,1)}, u32[]{:S(2)}, u32[]{:S(2)}) %collective-permute-start.15) | collective-permute-done | bytes 1048608 | tf_op jit(solution)/shard_map/ppermute | solution.py:659
  140.7 2.9 %own_spread.1.own_ref = f32[8,1,256]{2,1,0:T(1,128)} custom-call(bf16[8,256,512]{2,1,0:T(8,128)(2,1)} %get-tuple-element.14.refs_1_.obs_ref.refs_6_, bf16[14,4,256]{2,1,0:T(4,128)(2,1)} %pad_maximum_fusion.refs_2_.meta_ref, bf16[4096,128]{1,0:T(8,128)(2,1)} %collective-permute-done.15.refs_0_.refs_11_), custom_call_target="tpu_custom_call" | custom-call | flops 34538401792 | bytes 110700000 | tf_op jit(solution)/shard_map/own_spread/pallas_call | solution.py:180
  143.6 20.0 %collective-permute-done.14.after_ref.refs_5_ = bf16[2,3,256,512]{3,2,1,0:T(8,128)(2,1)} collective-permute-done((bf16[2,3,256,512]{3,2,1,0:T(8,128)(2,1)}, bf16[2,3,256,512]{3,2,1,0:T(8,128)(2,1)}, u32[]{:S(2)}, u32[]{:S(2)}) %collective-permute-start.14) | collective-permute-done | bytes 1572896 | tf_op jit(solution)/shard_map/ppermute | solution.py:674
  163.6 2.6 %all_spread.1.refs_2_ = f32[14,1,256]{2,1,0:T(1,128)} custom-call(bf16[2,3,256,512]{3,2,1,0:T(8,128)(2,1)} %copy-done.4, bf16[2,3,256,512]{3,2,1,0:T(8,128)(2,1)} %collective-permute-done.14.after_ref.refs_5_, f32[8,1,256]{2,1,0:T(1,128)} %own_spread.1.own_ref, bf16[14,4,256]{2,1,0:T(4,128)(2,1)} %pad_maximum_fusion.refs_2_.meta_ref), custom_call_target="tpu_custom_call" | custom-call | flops 4605120000 | bytes 14760000 | tf_op jit(solution)/shard_map/all_spread/pallas_call | solution.py:203
  166.2 10.8 %pairs.2.refs_13_ = f32[8,512,512]{2,1,0:T(8,128)} custom-call(s32[8,7]{1,0:T(8,128)} %refs_0_.21, f32[5,7,512,256]{3,2,1,0:T(8,128)} %taper.2.refs_3_.refs_1_, f32[14,1,256]{2,1,0:T(1,128)} %all_spread.1.refs_2_, bf16[8,2048,128]{2,1,0:T(8,128)(2,1)} %refs_3_.3, bf16[2,3,256,512]{3,2,1,0:T(8,128)(2,1)} %copy-done.4, ...), custom_call_target="tpu_custom_call" | custom-call | flops 17269200896 | bytes 55350000 | tf_op jit(solution)/shard_map/pairs/pallas_call | solution.py:390
  177.8 9.8 %pairs.3 = f32[8,512,512]{2,1,0:T(8,128)} custom-call(s32[8,7]{1,0:T(8,128)} %refs_0_.21, f32[3,7,512,256]{3,2,1,0:T(8,128)} %taper.3.refs_6_.refs_1_, f32[14,1,256]{2,1,0:T(1,128)} %all_spread.1.refs_2_, bf16[8,2048,128]{2,1,0:T(8,128)(2,1)} %refs_3_.3, bf16[2,3,256,512]{3,2,1,0:T(8,128)(2,1)} %copy-done.4, ...), custom_call_target="tpu_custom_call", output_to_operand_aliasing={{}: (13, {})} | custom-call | flops 10361520128 | bytes 33210000 | tf_op jit(solution)/shard_map/pairs/pallas_call | solution.py:390
  (54 shorter events, 20.0 us)
Async XLA Ops:
  0.0 34.7 %collective-permute-start = (bf16[8,256,128]{2,1,0:T(8,128)(2,1)}, bf16[8,256,128]{2,1,0:T(8,128)(2,1)}, u32[]{:S(2)}, u32[]{:S(2)}) collective-permute-start(bf16[8,256,128]{2,1,0:T(8,128)(2,1)} %refs_0_.14), channel_id=1, source_target_pairs={{0,1},{1,2},{2,3},{4,5},{5,6},{6,7},{8,9},{9,10},{10,11},{12,13},{... | collective-permute-start | bytes 1572872 | tf_op jit(solution)/shard_map/ppermute | solution.py:659
  4.8 31.2 %collective-permute-start.1 = (bf16[8,256,128]{2,1,0:T(8,128)(2,1)}, bf16[8,256,128]{2,1,0:T(8,128)(2,1)}, u32[]{:S(2)}, u32[]{:S(2)}) collective-permute-start(bf16[8,256,128]{2,1,0:T(8,128)(2,1)} %refs_0_.14), channel_id=1, source_target_pairs={{1,0},{2,1},{3,2},{5,4},{6,5},{7,6},{9,8},{10,9},{11,10},{13,12},{... | collective-permute-start | bytes 1572872 | tf_op jit(solution)/shard_map/ppermute | solution.py:659
  6.1 29.9 %collective-permute-start.2 = (bf16[8,256,128]{2,1,0:T(8,128)(2,1)}, bf16[8,256,128]{2,1,0:T(8,128)(2,1)}, u32[]{:S(2)}, u32[]{:S(2)}) collective-permute-start(bf16[8,256,128]{2,1,0:T(8,128)(2,1)} %refs_0_.14), channel_id=1, source_target_pairs={{0,2},{3,1},{4,6},{7,5},{8,10},{11,9},{12,14},{15,13},{16,18},{19,... | collective-permute-start | bytes 1572872 | tf_op jit(solution)/shard_map/ppermute | solution.py:659
  13.3 8.6 %copy-start.8 = (s32[8,256]{1,0:T(8,128)S(1)}, s32[8,256]{1,0:T(8,128)}, u32[]{:S(2)}) copy-start(s32[8,256]{1,0:T(8,128)} %param.11) | copy-start | bytes 24580
  13.3 9.9 %copy-start.7 = (bf16[2,8,2048]{2,1,0:T(8,128)(2,1)S(1)}, bf16[2,8,2048]{2,1,0:T(8,128)(2,1)}, u32[]{:S(2)}) copy-start(bf16[2,8,2048]{2,1,0:T(8,128)(2,1)} %param.10) | copy-start | bytes 196612
  13.3 42.1 %collective-permute-start.10 = (bf16[4096,128]{1,0:T(8,128)(2,1)}, bf16[4096,128]{1,0:T(8,128)(2,1)}, u32[]{:S(2)}, u32[]{:S(2)}) collective-permute-start(bf16[4096,128]{1,0:T(8,128)(2,1)} %cut.7), channel_id=1, source_target_pairs={{1,0},{2,1},{3,2},{5,4},{6,5},{7,6},{9,8},{10,9},{11,10},{13,12},{... | collective-permute-start | bytes 3145736 | tf_op jit(solution)/shard_map/ppermute | solution.py:659
  16.8 39.8 %collective-permute-start.9 = (bf16[4096,128]{1,0:T(8,128)(2,1)}, bf16[4096,128]{1,0:T(8,128)(2,1)}, u32[]{:S(2)}, u32[]{:S(2)}) collective-permute-start(bf16[4096,128]{1,0:T(8,128)(2,1)} %cut.6), channel_id=1, source_target_pairs={{0,1},{1,2},{2,3},{4,5},{5,6},{6,7},{8,9},{9,10},{10,11},{12,13},{... | collective-permute-start | bytes 3145736 | tf_op jit(solution)/shard_map/ppermute | solution.py:659
  23.9 8.8 %copy-start.9 = (bf16[8,256]{1,0:T(8,128)(2,1)S(1)}, bf16[8,256]{1,0:T(8,128)(2,1)}, u32[]{:S(2)}) copy-start(bf16[8,256]{1,0:T(8,128)(2,1)} %param.9) | copy-start | bytes 12292
  23.9 8.8 %copy-start.10 = (s32[8]{0:T(128)S(1)}, s32[8]{0:T(128)}, u32[]{:S(2)}) copy-start(s32[8]{0:T(128)} %param.12) | copy-start | bytes 100
  34.7 32.9 %collective-permute-start.6 = (bf16[8,256,128]{2,1,0:T(8,128)(2,1)}, bf16[8,256,128]{2,1,0:T(8,128)(2,1)S(1)}, u32[]{:S(2)}, u32[]{:S(2)}) collective-permute-start(bf16[8,256,128]{2,1,0:T(8,128)(2,1)} %get-tuple-element.11.refs_0_), channel_id=1, source_target_pairs={{0,1},{1,2},{2,3},{4,5},{5,6},{6,7},{8,9},{9,10},{10,11},{12,13},{... | collective-permute-start | bytes 1572872 | tf_op jit(solution)/shard_map/ppermute | solution.py:659
  39.6 15.1 %copy-start.6 = (bf16[8,4,256]{2,1,0:T(4,128)(2,1)S(1)}, bf16[8,4,256]{2,1,0:T(4,128)(2,1)}, u32[]{:S(2)}) copy-start(bf16[8,4,256]{2,1,0:T(4,128)(2,1)} %passed.1) | copy-start | bytes 49156
  40.4 8.5 %collective-permute-start.3 = (bf16[3,4,256]{2,1,0:T(4,128)(2,1)S(1)}, bf16[3,4,256]{2,1,0:T(4,128)(2,1)S(1)}, u32[]{:S(2)}, u32[]{:S(2)}) collective-permute-start(bf16[3,4,256]{2,1,0:T(4,128)(2,1)S(1)} %get-tuple-element.15), channel_id=1, source_target_pairs={{0,4},{4,8},{8,12},{12,16},{16,20},{20,24},{24,28},{1,5},{5,9},{9,... | collective-permute-start | bytes 18440 | tf_op jit(solution)/shard_map/ppermute | solution.py:674
  45.4 4.9 %collective-permute-start.4 = (bf16[3,4,256]{2,1,0:T(4,128)(2,1)S(1)}, bf16[3,4,256]{2,1,0:T(4,128)(2,1)S(1)}, u32[]{:S(2)}, u32[]{:S(2)}) collective-permute-start(bf16[3,4,256]{2,1,0:T(4,128)(2,1)S(1)} %get-tuple-element.16), channel_id=1, source_target_pairs={{4,0},{8,4},{12,8},{16,12},{20,16},{24,20},{28,24},{5,1},{9,5},{13... | collective-permute-start | bytes 18440 | tf_op jit(solution)/shard_map/ppermute | solution.py:674
  48.8 18.8 %collective-permute-start.7 = (bf16[8,256,128]{2,1,0:T(8,128)(2,1)}, bf16[8,256,128]{2,1,0:T(8,128)(2,1)S(1)}, u32[]{:S(2)}, u32[]{:S(2)}) collective-permute-start(bf16[8,256,128]{2,1,0:T(8,128)(2,1)} %get-tuple-element.11.refs_0_), channel_id=1, source_target_pairs={{1,0},{2,1},{3,2},{5,4},{6,5},{7,6},{9,8},{10,9},{11,10},{13,12},{... | collective-permute-start | bytes 1572872 | tf_op jit(solution)/shard_map/ppermute | solution.py:659
  50.4 20.8 %collective-permute-start.8 = (bf16[8,256,128]{2,1,0:T(8,128)(2,1)}, bf16[8,256,128]{2,1,0:T(8,128)(2,1)S(1)}, u32[]{:S(2)}, u32[]{:S(2)}) collective-permute-start(bf16[8,256,128]{2,1,0:T(8,128)(2,1)} %get-tuple-element.11.refs_0_), channel_id=1, source_target_pairs={{0,2},{3,1},{4,6},{7,5},{8,10},{11,9},{12,14},{15,13},{16,18},{19,... | collective-permute-start | bytes 1572872 | tf_op jit(solution)/shard_map/ppermute | solution.py:659
  55.3 31.1 %collective-permute-start.5 = (bf16[2,8,256,128]{3,2,1,0:T(8,128)(2,1)}, bf16[2,8,256,128]{3,2,1,0:T(8,128)(2,1)}, u32[]{:S(2)}, u32[]{:S(2)}) collective-permute-start(bf16[2,8,256,128]{3,2,1,0:T(8,128)(2,1)} %relay.2.refs_1_.refs_3_), channel_id=1, source_target_pairs={{2,3},{1,0},{6,7},{5,4},{10,11},{9,8},{14,15},{13,12},{18,19},{17,... | collective-permute-start | bytes 3145736 | tf_op jit(solution)/shard_map/ppermute | solution.py:663
  67.6 3.5 %copy-start.1 = (bf16[8,256,128]{2,1,0:T(8,128)(2,1)}, bf16[8,256,128]{2,1,0:T(8,128)(2,1)S(1)}, u32[]{:S(2)}) copy-start(bf16[8,256,128]{2,1,0:T(8,128)(2,1)S(1)} %collective-permute-done.6.refs_0_.refs_1_) | copy-start | bytes 1572868
  67.6 3.5 %copy-start.2 = (bf16[8,256,128]{2,1,0:T(8,128)(2,1)}, bf16[8,256,128]{2,1,0:T(8,128)(2,1)S(1)}, u32[]{:S(2)}) copy-start(bf16[8,256,128]{2,1,0:T(8,128)(2,1)S(1)} %collective-permute-done.7.refs_1_.refs_2_) | copy-start | bytes 1572868
  71.2 0.8 copy-start.3
  74.2 33.6 %collective-permute-start.11 = (bf16[2,8,256,128]{3,2,1,0:T(8,128)(2,1)}, bf16[2,8,256,128]{3,2,1,0:T(8,128)(2,1)}, u32[]{:S(2)}, u32[]{:S(2)}) collective-permute-start(bf16[2,8,256,128]{3,2,1,0:T(8,128)(2,1)} %relay.3.refs_5_.refs_1_), channel_id=1, source_target_pairs={{2,3},{1,0},{6,7},{5,4},{10,11},{9,8},{14,15},{13,12},{18,19},{17,... | collective-permute-start | bytes 3145736 | tf_op jit(solution)/shard_map/ppermute | solution.py:663
  77.6 29.4 %collective-permute-start.12 = (bf16[4096,128]{1,0:T(8,128)(2,1)}, bf16[4096,128]{1,0:T(8,128)(2,1)S(1)}, u32[]{:S(2)}, u32[]{:S(2)}) collective-permute-start(bf16[4096,128]{1,0:T(8,128)(2,1)} %cut.8), channel_id=1, source_target_pairs={{0,2},{3,1},{4,6},{7,5},{8,10},{11,9},{12,14},{15,13},{16,18},{19,... | collective-permute-start | bytes 3145736 | tf_op jit(solution)/shard_map/ppermute | solution.py:659
  107.0 1.0 copy-start
  115.0 25.6 %collective-permute-start.15 = (bf16[4096,128]{1,0:T(8,128)(2,1)}, bf16[4096,128]{1,0:T(8,128)(2,1)}, u32[]{:S(2)}, u32[]{:S(2)}) collective-permute-start(bf16[4096,128]{1,0:T(8,128)(2,1)} %cut.9), channel_id=1, source_target_pairs={{0,3},{3,0},{4,7},{7,4},{8,11},{11,8},{12,15},{15,12},{16,19},{19,... | collective-permute-start | bytes 3145736 | tf_op jit(solution)/shard_map/ppermute | solution.py:659
  119.3 24.3 %collective-permute-start.13 = (bf16[2,3,256,512]{3,2,1,0:T(8,128)(2,1)}, bf16[2,3,256,512]{3,2,1,0:T(8,128)(2,1)S(1)}, u32[]{:S(2)}, u32[]{:S(2)}) collective-permute-start(bf16[2,3,256,512]{3,2,1,0:T(8,128)(2,1)} %get-tuple-element.12), channel_id=1, source_target_pairs={{0,4},{4,8},{8,12},{12,16},{16,20},{20,24},{24,28},{1,5},{5,9},{9,... | collective-permute-start | bytes 4718600 | tf_op jit(solution)/shard_map/ppermute | solution.py:674
  125.4 38.2 %collective-permute-start.14 = (bf16[2,3,256,512]{3,2,1,0:T(8,128)(2,1)}, bf16[2,3,256,512]{3,2,1,0:T(8,128)(2,1)}, u32[]{:S(2)}, u32[]{:S(2)}) collective-permute-start(bf16[2,3,256,512]{3,2,1,0:T(8,128)(2,1)} %get-tuple-element.13), channel_id=1, source_target_pairs={{4,0},{8,4},{12,8},{16,12},{20,16},{24,20},{28,24},{5,1},{9,5},{13... | collective-permute-start | bytes 4718600 | tf_op jit(solution)/shard_map/ppermute | solution.py:674
  129.3 36.9 %collective-permute-start.17 = (bf16[2560,128]{1,0:T(8,128)(2,1)}, bf16[2560,128]{1,0:T(8,128)(2,1)}, u32[]{:S(2)}, u32[]{:S(2)}) collective-permute-start(bf16[2560,128]{1,0:T(8,128)(2,1)} %cut.11), channel_id=1, source_target_pairs={{1,3},{2,0},{5,7},{6,4},{9,11},{10,8},{13,15},{14,12},{17,19},{18,... | collective-permute-start | bytes 1966088 | tf_op jit(solution)/shard_map/ppermute | solution.py:659
  132.3 44.7 %collective-permute-start.16 = (bf16[1536,128]{1,0:T(8,128)(2,1)}, bf16[1536,128]{1,0:T(8,128)(2,1)S(1)}, u32[]{:S(2)}, u32[]{:S(2)}) collective-permute-start(bf16[1536,128]{1,0:T(8,128)(2,1)} %cut.10), channel_id=1, source_target_pairs={{1,3},{2,0},{5,7},{6,4},{9,11},{10,8},{13,15},{14,12},{17,19},{18,... | collective-permute-start | bytes 1179656 | tf_op jit(solution)/shard_map/ppermute | solution.py:659
  143.6 20.0 %copy-start.4 = (bf16[2,3,256,512]{3,2,1,0:T(8,128)(2,1)}, bf16[2,3,256,512]{3,2,1,0:T(8,128)(2,1)S(1)}, u32[]{:S(2)}) copy-start(bf16[2,3,256,512]{3,2,1,0:T(8,128)(2,1)S(1)} %collective-permute-done.13.before_ref.refs_4_) | copy-start | bytes 4718596
  177.0 0.8 copy-start.5
where the time goes:
time: 191 us; the launch traced here: 188 us
  Pallas kernels  81.7 us (43%)
  starting transfers between devices  57.8 us (30%)
  waiting for transfers between devices  39 us (20%)
  local copies, waits for them, and re-layouts  5.24 us (3%)
  other arithmetic  3.49 us (2%)
    ppermute x12, starting transfers between devices, hop(): return lax.ppermute(block, 'mem', pairs_of)  40.2 us
    pallas_call x2, Pallas kernels, tapers(): pl.pallas_call(functools.partial(taper_kernel, reach, first), grid=(here,...  21.2 us
    pallas_call x2, Pallas kernels, pairs(): pl.pallas_call(functools.partial(pair_kernel, first, reach, here, parts,...  20.6 us
    ppermute x4, waiting for transfers between devices, halo(): return (lax.ppermute(last, 'dist', up), lax.ppermute(first, 'dist', down))  20.3 us
    ppermute x12, waiting for transfers between devices, hop(): return lax.ppermute(block, 'mem', pairs_of)  18 us
    ppermute x4, starting transfers between devices, halo(): return (lax.ppermute(last, 'dist', up), lax.ppermute(first, 'dist', down))  15 us
    pallas_call x6, Pallas kernels, cut(): pl.pallas_call(functools.partial(cut_kernel, start, targets, more), in_sp...  12.1 us
    pallas_call x1, Pallas kernels, pick(): pl.pallas_call(pick_kernel, grid=(count,), in_specs=[pl.BlockSpec((1, slo...  8.76 us
  transfers between devices with their start and end apart: 18, of which 6 were waited for; matrix products, arithmetic and copies ran while one was open for 4% of the time, Pallas kernels for 35%

commit v1 on v0

--- a/solution.py
+++ b/solution.py
@@ -12,7 +12,7 @@
 SPREAD_COST = 30
 PACE = 1.0
 WHOLE = pl.BlockSpec(memory_space=pltpu.HBM)
-CHUNKS = (5, 3)
+CHUNKS = (4, 4)
 
 
 def params(**more):
@@ -189,43 +189,32 @@
 
 
 def all_spread_kernel(degrees, before_ref, after_ref, own_ref, meta_ref, out_ref):
-    reach, count = before_ref.shape[1], own_ref.shape[0]
+    reach, count = before_ref.shape[0], own_ref.shape[0]
     out_ref[reach : reach + count] = own_ref[...]
     for d in range(reach):
-        out_ref[d] = spread_row(before_ref[0, d], meta_ref[d], degrees)
+        out_ref[d] = spread_row(before_ref[d], meta_ref[d], degrees)
         e = reach + count + d
-        out_ref[e] = spread_row(after_ref[0, d], meta_ref[e], degrees)
-
-
-def all_spread(edges, own, meta):
-    _, reach, slots, members = edges[0].shape
-    edge = pl.BlockSpec((1, reach, slots, members), lambda i: (1, 0, 0, 0))
+        out_ref[e] = spread_row(after_ref[d], meta_ref[e], degrees)
+
+
+def all_spread(before, after, own, meta):
+    slots, members = before.shape[1:]
     return pl.pallas_call(
         functools.partial(all_spread_kernel, float(members - 1)),
-        grid=(1,),
-        in_specs=[
-            edge,
-            edge,
-            pl.BlockSpec(own.shape, lambda i: (0, 0, 0)),
-            pl.BlockSpec(meta.shape, lambda i: (0, 0, 0)),
-        ],
-        out_specs=pl.BlockSpec((meta.shape[0], 1, slots), lambda i: (0, 0, 0)),
         out_shape=jax.ShapeDtypeStruct((meta.shape[0], 1, slots), F32),
         compiler_params=params(),
         cost_estimate=cost(4),
         name="all_spread",
-    )(*edges, own, meta)
+    )(before, after, own, meta)
 
 
 def pair_kernel(first, reach, here, parts, routes, bases, *refs):
     flags_ref, taper_ref, scale_ref, table_ref = refs[:4]
-    before_ref, after_ref, obs_ref, innov_ref = refs[4:8]
-    obs_refs = (before_ref.at[1], obs_ref, after_ref.at[1])
-    innov_refs = (before_ref.at[0], innov_ref, after_ref.at[0])
-    piece_refs = refs[8 : 8 + len(bases)]
+    obs_refs, innov_refs = refs[4:7], refs[7:10]
+    piece_refs = refs[10 : 10 + len(bases)]
     out_ref, x_buf, t_buf, obs_buf, innov_buf, total, x_sem, sem, out_sem = refs[-9:]
     rows, width = table_ref.shape[1] // parts, table_ref.shape[2]
-    own, slots = obs_ref.shape[:2]
+    own, slots = obs_refs[1].shape[:2]
     me = lax.axis_index("mem")
 
     def band(index):
@@ -367,20 +356,20 @@
         out_copy(index).wait()
 
 
-def pairs(first, flags, taper, scale, table, pieces, routes, edges, obs, innov, out):
+def pairs(first, flags, taper, scale, table, pieces, routes, obs, innov, out):
     count = table.shape[0]
     here, _, rows, _ = taper.shape
     parts = table.shape[1] // rows
     bases = [base for _, base in pieces]
-    slots, members = obs.shape[1:]
+    slots, members = obs[1].shape[1:]
     slot_count = flags.shape[1]
     reach = (slot_count - 1) // 2
-    operands = [flags, taper, scale, table, *edges, obs, innov, *[array for array, _ in pieces]]
+    operands = [flags, taper, scale, table, *obs, *innov, *[array for array, _ in pieces]]
     in_specs = [
         pl.BlockSpec(memory_space=pltpu.SMEM),
         WHOLE,
         pl.BlockSpec(memory_space=pltpu.VMEM),
-        *[WHOLE] * (5 + len(pieces)),
+        *[WHOLE] * (7 + len(pieces)),
     ]
     aliases = {}
     if out is not None:
@@ -555,17 +544,8 @@
     own, p1, p2, p3, far = refs[:5]
     me = lax.axis_index("mem")
     count, slots, width = own.shape
-    if edges:
-        other = refs[5]
-        out_ref, last_ref, first_ref, buf, edge, sem, edge_sem = refs[-7:]
-        sides = [(first_ref, 0), (last_ref, count - edges)]
-        for n, (_, at) in enumerate(sides):
-            pltpu.make_async_copy(
-                other.at[at : at + edges], edge.at[n], edge_sem.at[0, n]
-            ).start()
-    else:
-        out_ref, buf, sem = refs[-3:]
-        sides = []
+    out_ref, last_ref, first_ref, buf, sem = refs[-5:]
+    sides = [(first_ref, 0), (last_ref, count - edges)]
     p4, p5 = far.at[0], far.at[1]
     table = (
         (own, p2, p4, p5),
@@ -593,35 +573,27 @@
                     ))
             move(copies)
 
-    copies = []
-    for n, (side_ref, at) in enumerate(sides):
-        pltpu.make_async_copy(other.at[at : at + edges], edge.at[n], edge_sem.at[0, n]).wait()
-        copies.append(pltpu.make_async_copy(edge.at[n], side_ref.at[0], edge_sem.at[1, n]))
-        for d in range(edges):
-            for j in range(4):
-                copies.append(
-                    pltpu.make_async_copy(
-                        buf.at[j, at + d],
-                        side_ref.at[1, d, :, j * width : (j + 1) * width],
-                        sem.at[n, j, d],
-                    )
-                )
+    copies = [
+        pltpu.make_async_copy(
+            buf.at[j, at + d], side_ref.at[d, :, j * width : (j + 1) * width], sem.at[n, j, d]
+        )
+        for n, (side_ref, at) in enumerate(sides)
+        for d in range(edges)
+        for j in range(4)
+    ]
     for copy in copies:
         copy.start()
     for copy in copies:
         copy.wait()
 
 
-def place(own, near, far, edges, after):
+def place(own, near, far, edges, after, length):
     count, slots, width = own.shape
     operands = (own, *near, far, *after)
     shapes = [jax.ShapeDtypeStruct((count, slots, 4 * width), BF)]
+    shapes += [jax.ShapeDtypeStruct((edges, slots, 4 * width), BF)] * 2
     scratch = [pltpu.VMEM((4, count, slots, width), BF)]
     sems = [pltpu.SemaphoreType.DMA((2, 4, count))]
-    if edges:
-        shapes += [jax.ShapeDtypeStruct((2, edges, slots, 4 * width), BF)] * 2
-        scratch.append(pltpu.VMEM((2, edges, slots, 4 * width), BF))
-        sems.append(pltpu.SemaphoreType.DMA((2, 2)))
     return pl.pallas_call(
         functools.partial(place_kernel, edges),
         in_specs=[WHOLE] * len(operands),
@@ -629,7 +601,7 @@
         out_shape=shapes,
         scratch_shapes=scratch + sems,
         compiler_params=params(),
-        cost_estimate=cost(0.1 if edges else 3),
+        cost_estimate=cost(length),
         name="place",
     )(*operands)
 
@@ -715,13 +687,16 @@
         relay_obs = relay(*near_obs, (taper[0],))
         far_obs = last_hop(relay_obs)
         middle = hop(cut(anomalies, 0, count, (2, 2, 1, 1), None, (relay_obs,)), far_pairs)
-        (full_innov,) = place(innovations, near_innov, far_innov, 0, (relay_obs,))
+        full_innov, last, first = place(innovations, near_innov, far_innov, reach, (relay_obs,), 3)
+        low, high = halo(last, first)
+        all_innov = (low, full_innov, high)
         weigh(1, full_innov)
+        end_block = cut(anomalies, 0, count, through, None, (full_innov,), 0.1)
         full_obs, last, first = place(
-            observed, near_obs, far_obs, reach, (full_innov, taper[1], middle)
-        )
-        edges = halo(last, first)
-        end_block = cut(anomalies, 0, count, through, None, (full_obs,), 0.1)
+            observed, near_obs, far_obs, reach, (taper[1], middle, low, high), 0.1
+        )
+        low, high = halo(last, first)
+        all_obs = (low, full_obs, high)
         ends = hop(end_block, ((0, 3), (3, 0)))
         cross = [
             hop(cut(anomalies, start, here, through, None, (full_obs,), 0.1), ((1, 3), (2, 0)))
@@ -744,8 +719,11 @@
         ext_meta = jnp.concatenate([meta_before, meta, meta_after], axis=0)
         full_innov = lax.all_gather(innovations, "mem", axis=2, tiled=True)
         full_obs = lax.all_gather(observed, "mem", axis=2, tiled=True)
-        both = jnp.stack([full_innov, full_obs])
-        edges = halo(both[:, -reach:], both[:, :reach])
+        all_innov, all_obs = [
+            (low, full, high)
+            for full in (full_innov, full_obs)
+            for low, high in [halo(full[-reach:], full[:reach])]
+        ]
         pieces = []
         for c, (first, size) in enumerate(zip(starts, chunks)):
             weigh(c)
@@ -765,7 +743,7 @@
         }
     if parts != 4:
         own_scale = own_spread(full_obs, ext_meta, reach, ())
-    scale = all_spread(edges, own_scale, ext_meta)
+    scale = all_spread(all_obs[0], all_obs[2], own_scale, ext_meta)
 
     out = None
     for c in range(len(chunks)):
@@ -777,9 +755,8 @@
             anomalies,
             pieces[c],
             routes,
-            edges,
-            full_obs,
-            full_innov,
+            all_obs,
+            all_innov,
             out,
         )
     return out

time: 191 us -> 178 us (0.932)
  waiting for transfers between devices: 39 us -> 11.7 us
  Pallas kernels: 81.7 us -> 90.3 us
  starting transfers between devices: 57.8 us -> 62.9 us
    ppermute x12, waiting for transfers between devices: 18 us -> 3.03 us  [hop(): return lax.ppermute(block, 'mem', pairs_of)]
    ppermute x4 -> x6, waiting for transfers between devices: 20.3 us -> 8.65 us  [halo(): return (lax.ppermute(last, 'dist', up), lax.ppermute(first, 'dist', down))]
    ppermute x4 -> x6, starting transfers between devices: 15 us -> 20.6 us  [halo(): return (lax.ppermute(last, 'dist', up), lax.ppermute(first, 'dist', down))]
    pallas_call x2, Pallas kernels: 21.2 us -> 26 us  [tapers(): pl.pallas_call(functools.partial(taper_kernel, reach, first), grid=(here,...]
    pallas_call x2, Pallas kernels: 20.6 us -> 24.1 us  [pairs(): pl.pallas_call(functools.partial(pair_kernel, first, reach, here, parts,...]
  transfers between devices with their start and end apart: 18 -> 20, of which waited for: 6 -> 3; matrix products, arithmetic and copies ran while one was open for 4% -> 4% of each run, Pallas kernels for 35% -> 44%
where the time goes in v1:
time: 178 us; the launch traced here: 176 us
  Pallas kernels  90.3 us (51%)
  starting transfers between devices  62.9 us (35%)
  waiting for transfers between devices  11.7 us (7%)
  local copies, waits for them, and re-layouts  6.19 us (3%)
  other arithmetic  4.21 us (2%)
    ppermute x12, starting transfers between devices, hop(): return lax.ppermute(block, 'mem', pairs_of)  39.7 us
    pallas_call x2, Pallas kernels, tapers(): pl.pallas_call(functools.partial(taper_kernel, reach, first), grid=(here,...  26 us
    pallas_call x2, Pallas kernels, pairs(): pl.pallas_call(functools.partial(pair_kernel, first, reach, here, parts,...  24.1 us
    ppermute x6, starting transfers between devices, halo(): return (lax.ppermute(last, 'dist', up), lax.ppermute(first, 'dist', down))  20.6 us
    pallas_call x6, Pallas kernels, cut(): pl.pallas_call(functools.partial(cut_kernel, start, targets, more), in_sp...  12.2 us
    pallas_call x1, Pallas kernels, pick(): pl.pallas_call(pick_kernel, grid=(count,), in_specs=[pl.BlockSpec((1, slo...  8.75 us
    ppermute x6, waiting for transfers between devices, halo(): return (lax.ppermute(last, 'dist', up), lax.ppermute(first, 'dist', down))  8.65 us
    pallas_call x2, Pallas kernels, place(): pl.pallas_call(functools.partial(place_kernel, edges), in_specs=[WHOLE] *...  7.97 us
  transfers between devices with their start and end apart: 20, of which 3 were waited for; matrix products, arithmetic and copies ran while one was open for 4% of the time, Pallas kernels for 44%

profile of v1, /device:TPU:1, one launch (start us, length us, event | category | flops | bytes accessed | tf_op | source)
XLA Modules:
  0.0 175.7 jit_solution(11320107524674234624)
XLA Ops:
  0.0 4.8 %collective-permute-start = (bf16[8,256,128]{2,1,0:T(8,128)(2,1)}, bf16[8,256,128]{2,1,0:T(8,128)(2,1)}, u32[]{:S(2)}, u32[]{:S(2)}) collective-permute-start(bf16[8,256,128]{2,1,0:T(8,128)(2,1)} %refs_0_.14), channel_id=1, source_target_pairs={{0,1},{1,2},{2,3},{4,5},{5,6},{6,7},{8,9},{9,10},{10,11},{12,13},{... | collective-permute-start | bytes 1572872 | tf_op jit(solution)/shard_map/ppermute | solution.py:631
  6.1 5.0 %collective-permute-start.2 = (bf16[8,256,128]{2,1,0:T(8,128)(2,1)}, bf16[8,256,128]{2,1,0:T(8,128)(2,1)}, u32[]{:S(2)}, u32[]{:S(2)}) collective-permute-start(bf16[8,256,128]{2,1,0:T(8,128)(2,1)} %refs_0_.14), channel_id=1, source_target_pairs={{0,2},{3,1},{4,6},{7,5},{8,10},{11,9},{12,14},{15,13},{16,18},{19,... | collective-permute-start | bytes 1572872 | tf_op jit(solution)/shard_map/ppermute | solution.py:631
  11.2 2.1 %cut.7 = bf16[4096,128]{1,0:T(8,128)(2,1)} custom-call(bf16[8,2048,128]{2,1,0:T(8,128)(2,1)} %refs_3_.3), custom_call_target="tpu_custom_call" | custom-call | flops 2302560000 | bytes 7380000 | tf_op jit(solution)/shard_map/cut/pallas_call | solution.py:467
  14.7 2.1 %cut.6 = bf16[4096,128]{1,0:T(8,128)(2,1)} custom-call(bf16[8,2048,128]{2,1,0:T(8,128)(2,1)} %refs_3_.3), custom_call_target="tpu_custom_call" | custom-call | flops 2302560000 | bytes 7380000 | tf_op jit(solution)/shard_map/cut/pallas_call | solution.py:467
  16.8 5.0 %collective-permute-start.9 = (bf16[4096,128]{1,0:T(8,128)(2,1)}, bf16[4096,128]{1,0:T(8,128)(2,1)}, u32[]{:S(2)}, u32[]{:S(2)}) collective-permute-start(bf16[4096,128]{1,0:T(8,128)(2,1)} %cut.6), channel_id=1, source_target_pairs={{0,1},{1,2},{2,3},{4,5},{5,6},{6,7},{8,9},{9,10},{10,11},{12,13},{... | collective-permute-start | bytes 3145736 | tf_op jit(solution)/shard_map/ppermute | solution.py:631
  23.9 8.8 %pick.1 = (bf16[8,256,128]{2,1,0:T(8,128)(2,1)}, bf16[8,2,256]{2,1,0:T(2,128)(2,1)}) custom-call(s32[8,256,1]{2,1,0:T(8,128)} %copy.13.node_ref, bf16[8,2048,128]{2,1,0:T(8,128)(2,1)} %refs_3_.3, bf16[8,2,2048]{2,1,0:T(2,128)(2,1)} %bitcast.7), custom_call_target="tpu_custom_call" | custom-call | flops 8058959872 | bytes 25830000 | tf_op jit(solution)/shard_map/pick/pallas_call | solution.py:41
  36.0 2.2 %relay.2.refs_1_.refs_3_ = bf16[2,8,256,128]{3,2,1,0:T(8,128)(2,1)} custom-call(bf16[8,256,128]{2,1,0:T(8,128)(2,1)} %collective-permute-done.refs_0_.refs_1_, bf16[8,256,128]{2,1,0:T(8,128)(2,1)} %collective-permute-done.1.refs_1_.refs_2_, bf16[8,256,128]{2,1,0:T(8,128)(2,1)} %collective-permute-done.2.refs_2_.refs_3_), custom_call_target="tpu_custom_call" | custom-call | flops 2302560000 | bytes 7380000 | tf_op jit(solution)/shard_map/relay/pallas_call | solution.py:412
  40.2 5.1 %collective-permute-start.3 = (bf16[3,4,256]{2,1,0:T(4,128)(2,1)S(1)}, bf16[3,4,256]{2,1,0:T(4,128)(2,1)S(1)}, u32[]{:S(2)}, u32[]{:S(2)}) collective-permute-start(bf16[3,4,256]{2,1,0:T(4,128)(2,1)S(1)} %get-tuple-element.21), channel_id=1, source_target_pairs={{0,4},{4,8},{8,12},{12,16},{16,20},{20,24},{24,28},{1,5},{5,9},{9,... | collective-permute-start | bytes 18440 | tf_op jit(solution)/shard_map/ppermute | solution.py:646
  45.3 1.9 %collective-permute-start.4 = (bf16[3,4,256]{2,1,0:T(4,128)(2,1)S(1)}, bf16[3,4,256]{2,1,0:T(4,128)(2,1)S(1)}, u32[]{:S(2)}, u32[]{:S(2)}) collective-permute-start(bf16[3,4,256]{2,1,0:T(4,128)(2,1)S(1)} %get-tuple-element.22), channel_id=1, source_target_pairs={{4,0},{8,4},{12,8},{16,12},{20,16},{24,20},{28,24},{5,1},{9,5},{13... | collective-permute-start | bytes 18440 | tf_op jit(solution)/shard_map/ppermute | solution.py:646
  47.2 1.5 convert_bitcast_fusion.refs_1_
  50.3 4.4 %collective-permute-start.8 = (bf16[8,256,128]{2,1,0:T(8,128)(2,1)}, bf16[8,256,128]{2,1,0:T(8,128)(2,1)S(1)}, u32[]{:S(2)}, u32[]{:S(2)}) collective-permute-start(bf16[8,256,128]{2,1,0:T(8,128)(2,1)} %get-tuple-element.14.refs_0_), channel_id=1, source_target_pairs={{0,2},{3,1},{4,6},{7,5},{8,10},{11,9},{12,14},{15,13},{16,18},{19,... | collective-permute-start | bytes 1572872 | tf_op jit(solution)/shard_map/ppermute | solution.py:631
  57.3 10.8 %taper.2.refs_3_.refs_1_ = f32[4,7,512,256]{3,2,1,0:T(8,128)} custom-call(s32[8,7]{1,0:T(8,128)} %refs_0_.21, f32[8,512,2]{2,1,0:T(8,128)} %convert_bitcast_fusion.refs_1_, bf16[14,4,256]{2,1,0:T(4,128)(2,1)} %pad_maximum_fusion.refs_2_.meta_ref, bf16[2,8,256,128]{3,2,1,0:T(8,128)(2,1)} %relay.2.refs_1_.refs_3_, ...), custom_call_target="tpu_custom_call" | custom-call | flops 13815359488 | bytes 44280000 | tf_op jit(solution)/shard_map/taper/pallas_call | solution.py:132
  68.2 3.0 %collective-permute-done.8.refs_2_.refs_3_ = bf16[8,256,128]{2,1,0:T(8,128)(2,1)S(1)} collective-permute-done((bf16[8,256,128]{2,1,0:T(8,128)(2,1)}, bf16[8,256,128]{2,1,0:T(8,128)(2,1)S(1)}, u32[]{:S(2)}, u32[]{:S(2)}) %collective-permute-start.8) | collective-permute-done | bytes 524320 | tf_op jit(solution)/shard_map/ppermute | solution.py:631
  72.0 2.2 %relay.3.refs_5_.refs_1_ = bf16[2,8,256,128]{3,2,1,0:T(8,128)(2,1)} custom-call(bf16[8,256,128]{2,1,0:T(8,128)(2,1)} %copy-done, bf16[8,256,128]{2,1,0:T(8,128)(2,1)} %copy-done.1, bf16[8,256,128]{2,1,0:T(8,128)(2,1)} %copy-done.2, f32[4,7,512,256]{3,2,1,0:T(8,128)} %taper.2.refs_3_.refs_1_), custom_call_target="tpu_custom_call" | custom-call | flops 2302560000 | bytes 7380000 | tf_op jit(solution)/shard_map/relay/pallas_call | solution.py:412
  75.4 2.1 %cut.8 = bf16[4096,128]{1,0:T(8,128)(2,1)} custom-call(bf16[8,2048,128]{2,1,0:T(8,128)(2,1)} %refs_3_.3, bf16[2,8,256,128]{3,2,1,0:T(8,128)(2,1)} %relay.3.refs_5_.refs_1_), custom_call_target="tpu_custom_call" | custom-call | flops 2302560000 | bytes 7380000 | tf_op jit(solution)/shard_map/cut/pallas_call | solution.py:467
  77.6 8.9 %collective-permute-start.12 = (bf16[4096,128]{1,0:T(8,128)(2,1)}, bf16[4096,128]{1,0:T(8,128)(2,1)S(1)}, u32[]{:S(2)}, u32[]{:S(2)}) collective-permute-start(bf16[4096,128]{1,0:T(8,128)(2,1)} %cut.8), channel_id=1, source_target_pairs={{0,2},{3,1},{4,6},{7,5},{8,10},{11,9},{12,14},{15,13},{16,18},{19,... | collective-permute-start | bytes 3145736 | tf_op jit(solution)/shard_map/ppermute | solution.py:631
  86.5 4.0 %place.2 = (bf16[8,256,512]{2,1,0:T(8,128)(2,1)}, bf16[3,256,512]{2,1,0:T(8,128)(2,1)}, bf16[3,256,512]{2,1,0:T(8,128)(2,1)}) custom-call(bf16[8,256,128]{2,1,0:T(8,128)(2,1)} %refs_0_.14, bf16[8,256,128]{2,1,0:T(8,128)(2,1)} %collective-permute-done.refs_0_.refs_1_, bf16[8,256,128]{2,1,0:T(8,128)(2,1)} %collective-permute-done.1.refs_1_.refs_2_, ...), custom_call_target="tpu_custom_call" | custom-call | flops 3453839872 | bytes 11070000 | tf_op jit(solution)/shard_map/place/pallas_call | solution.py:597
  90.5 5.4 %collective-permute-start.13 = (bf16[3,256,512]{2,1,0:T(8,128)(2,1)}, bf16[3,256,512]{2,1,0:T(8,128)(2,1)S(1)}, u32[]{:S(2)}, u32[]{:S(2)}) collective-permute-start(bf16[3,256,512]{2,1,0:T(8,128)(2,1)} %get-tuple-element.16), channel_id=1, source_target_pairs={{0,4},{4,8},{8,12},{12,16},{16,20},{20,24},{24,28},{1,5},{5,9},{9,... | collective-permute-start | bytes 2359304 | tf_op jit(solution)/shard_map/ppermute | solution.py:646
  96.0 1.9 %collective-permute-start.14 = (bf16[3,256,512]{2,1,0:T(8,128)(2,1)}, bf16[3,256,512]{2,1,0:T(8,128)(2,1)}, u32[]{:S(2)}, u32[]{:S(2)}) collective-permute-start(bf16[3,256,512]{2,1,0:T(8,128)(2,1)} %get-tuple-element.17), channel_id=1, source_target_pairs={{4,0},{8,4},{12,8},{16,12},{20,16},{24,20},{28,24},{5,1},{9,5},{13... | collective-permute-start | bytes 2359304 | tf_op jit(solution)/shard_map/ppermute | solution.py:646
  97.9 2.2 %cut.9 = bf16[4096,128]{1,0:T(8,128)(2,1)} custom-call(bf16[8,2048,128]{2,1,0:T(8,128)(2,1)} %refs_3_.3, bf16[8,256,512]{2,1,0:T(8,128)(2,1)} %get-tuple-element.15.refs_3_.refs_1_.refs_8_), custom_call_target="tpu_custom_call" | custom-call | flops 115128000 | bytes 369000 | tf_op jit(solution)/shard_map/cut/pallas_call | solution.py:467
  100.1 3.7 %collective-permute-start.17 = (bf16[4096,128]{1,0:T(8,128)(2,1)}, bf16[4096,128]{1,0:T(8,128)(2,1)}, u32[]{:S(2)}, u32[]{:S(2)}) collective-permute-start(bf16[4096,128]{1,0:T(8,128)(2,1)} %cut.9), channel_id=1, source_target_pairs={{0,3},{3,0},{4,7},{7,4},{8,11},{11,8},{12,15},{15,12},{16,19},{19,... | collective-permute-start | bytes 3145736 | tf_op jit(solution)/shard_map/ppermute | solution.py:631
  103.8 15.2 %taper.3.refs_5_.refs_1_ = f32[4,7,512,256]{3,2,1,0:T(8,128)} custom-call(s32[8,7]{1,0:T(8,128)} %refs_0_.21, f32[8,512,2]{2,1,0:T(8,128)} %convert_bitcast_fusion.refs_1_, bf16[14,4,256]{2,1,0:T(4,128)(2,1)} %pad_maximum_fusion.refs_2_.meta_ref, bf16[8,256,512]{2,1,0:T(8,128)(2,1)} %get-tuple-element.15.refs_3_.refs_1_.refs_8_), custom_call_target="tpu_custom_call" | custom-call | flops 13815359488 | bytes 44280000 | tf_op jit(solution)/shard_map/taper/pallas_call | solution.py:132
  120.2 3.9 %place.3 = (bf16[8,256,512]{2,1,0:T(8,128)(2,1)}, bf16[3,256,512]{2,1,0:T(8,128)(2,1)}, bf16[3,256,512]{2,1,0:T(8,128)(2,1)}) custom-call(bf16[8,256,128]{2,1,0:T(8,128)(2,1)} %get-tuple-element.14.refs_0_, bf16[8,256,128]{2,1,0:T(8,128)(2,1)} %copy-done, bf16[8,256,128]{2,1,0:T(8,128)(2,1)} %copy-done.1, bf16[8,256,128]{2,1,0:T(8,128)(2,1)} %copy-done.2, ...), custom_call_target="tpu_custom_call" | custom-call | flops 115128000 | bytes 369000 | tf_op jit(solution)/shard_map/place/pallas_call | solution.py:597
  124.2 4.3 %collective-permute-start.15 = (bf16[3,256,512]{2,1,0:T(8,128)(2,1)}, bf16[3,256,512]{2,1,0:T(8,128)(2,1)S(1)}, u32[]{:S(2)}, u32[]{:S(2)}) collective-permute-start(bf16[3,256,512]{2,1,0:T(8,128)(2,1)} %get-tuple-element.18), channel_id=1, source_target_pairs={{0,4},{4,8},{8,12},{12,16},{16,20},{20,24},{24,28},{1,5},{5,9},{9,... | collective-permute-start | bytes 2359304 | tf_op jit(solution)/shard_map/ppermute | solution.py:646
  128.5 1.9 %collective-permute-start.16 = (bf16[3,256,512]{2,1,0:T(8,128)(2,1)}, bf16[3,256,512]{2,1,0:T(8,128)(2,1)S(1)}, u32[]{:S(2)}, u32[]{:S(2)}) collective-permute-start(bf16[3,256,512]{2,1,0:T(8,128)(2,1)} %get-tuple-element.19), channel_id=1, source_target_pairs={{4,0},{8,4},{12,8},{16,12},{20,16},{24,20},{28,24},{5,1},{9,5},{13... | collective-permute-start | bytes 2359304 | tf_op jit(solution)/shard_map/ppermute | solution.py:646
  130.5 1.9 %cut.11 = bf16[2048,128]{1,0:T(8,128)(2,1)} custom-call(bf16[8,2048,128]{2,1,0:T(8,128)(2,1)} %refs_3_.3, bf16[8,256,512]{2,1,0:T(8,128)(2,1)} %get-tuple-element.20.obs_ref.refs_1_.refs_5_), custom_call_target="tpu_custom_call" | custom-call | flops 115128000 | bytes 369000 | tf_op jit(solution)/shard_map/cut/pallas_call | solution.py:467
  133.6 1.8 %cut.10 = bf16[2048,128]{1,0:T(8,128)(2,1)} custom-call(bf16[8,2048,128]{2,1,0:T(8,128)(2,1)} %refs_3_.3, bf16[8,256,512]{2,1,0:T(8,128)(2,1)} %get-tuple-element.20.obs_ref.refs_1_.refs_5_), custom_call_target="tpu_custom_call" | custom-call | flops 115128000 | bytes 369000 | tf_op jit(solution)/shard_map/cut/pallas_call | solution.py:467
  136.8 2.9 %own_spread.1.own_ref = f32[8,1,256]{2,1,0:T(1,128)} custom-call(bf16[8,256,512]{2,1,0:T(8,128)(2,1)} %get-tuple-element.20.obs_ref.refs_1_.refs_5_, bf16[14,4,256]{2,1,0:T(4,128)(2,1)} %pad_maximum_fusion.refs_2_.meta_ref, bf16[4096,128]{1,0:T(8,128)(2,1)} %collective-permute-done.17.refs_0_.refs_13_), custom_call_target="tpu_custom_call" | custom-call | flops 34538401792 | bytes 110700000 | tf_op jit(solution)/shard_map/own_spread/pallas_call | solution.py:180
  139.7 8.4 %collective-permute-done.16.after_ref.refs_6_ = bf16[3,256,512]{2,1,0:T(8,128)(2,1)S(1)} collective-permute-done((bf16[3,256,512]{2,1,0:T(8,128)(2,1)}, bf16[3,256,512]{2,1,0:T(8,128)(2,1)S(1)}, u32[]{:S(2)}, u32[]{:S(2)}) %collective-permute-start.16) | collective-permute-done | bytes 786464 | tf_op jit(solution)/shard_map/ppermute | solution.py:646
  149.0 2.6 %all_spread.1.refs_2_ = f32[14,1,256]{2,1,0:T(1,128)} custom-call(bf16[3,256,512]{2,1,0:T(8,128)(2,1)} %copy-done.9, bf16[3,256,512]{2,1,0:T(8,128)(2,1)} %copy-done.10, f32[8,1,256]{2,1,0:T(1,128)} %own_spread.1.own_ref, bf16[14,4,256]{2,1,0:T(4,128)(2,1)} %pad_maximum_fusion.refs_2_.meta_ref), custom_call_target="tpu_custom_call" | custom-call | flops 4605120000 | bytes 14760000 | tf_op jit(solution)/shard_map/all_spread/pallas_call | solution.py:202
  151.5 10.3 %pairs.2.refs_15_ = f32[8,512,512]{2,1,0:T(8,128)} custom-call(s32[8,7]{1,0:T(8,128)} %refs_0_.21, f32[4,7,512,256]{3,2,1,0:T(8,128)} %taper.2.refs_3_.refs_1_, f32[14,1,256]{2,1,0:T(1,128)} %all_spread.1.refs_2_, bf16[8,2048,128]{2,1,0:T(8,128)(2,1)} %refs_3_.3, bf16[3,256,512]{2,1,0:T(8,128)(2,1)} %copy-done.9, ...), custom_call_target="tpu_custom_call" | custom-call | flops 13815359488 | bytes 44280000 | tf_op jit(solution)/shard_map/pairs/pallas_call | solution.py:379
  161.9 13.8 %pairs.3 = f32[8,512,512]{2,1,0:T(8,128)} custom-call(s32[8,7]{1,0:T(8,128)} %refs_0_.21, f32[4,7,512,256]{3,2,1,0:T(8,128)} %taper.3.refs_5_.refs_1_, f32[14,1,256]{2,1,0:T(1,128)} %all_spread.1.refs_2_, bf16[8,2048,128]{2,1,0:T(8,128)(2,1)} %refs_3_.3, bf16[3,256,512]{2,1,0:T(8,128)(2,1)} %copy-done.9, ...), custom_call_target="tpu_custom_call", output_to_operand_aliasing={{}: (15, {})} | custom-call | flops 13815359488 | bytes 44280000 | tf_op jit(solution)/shard_map/pairs/pallas_call | solution.py:379
  (58 shorter events, 21.0 us)
Async XLA Ops:
  0.0 34.6 %collective-permute-start = (bf16[8,256,128]{2,1,0:T(8,128)(2,1)}, bf16[8,256,128]{2,1,0:T(8,128)(2,1)}, u32[]{:S(2)}, u32[]{:S(2)}) collective-permute-start(bf16[8,256,128]{2,1,0:T(8,128)(2,1)} %refs_0_.14), channel_id=1, source_target_pairs={{0,1},{1,2},{2,3},{4,5},{5,6},{6,7},{8,9},{9,10},{10,11},{12,13},{... | collective-permute-start | bytes 1572872 | tf_op jit(solution)/shard_map/ppermute | solution.py:631
  4.8 31.1 %collective-permute-start.1 = (bf16[8,256,128]{2,1,0:T(8,128)(2,1)}, bf16[8,256,128]{2,1,0:T(8,128)(2,1)}, u32[]{:S(2)}, u32[]{:S(2)}) collective-permute-start(bf16[8,256,128]{2,1,0:T(8,128)(2,1)} %refs_0_.14), channel_id=1, source_target_pairs={{1,0},{2,1},{3,2},{5,4},{6,5},{7,6},{9,8},{10,9},{11,10},{13,12},{... | collective-permute-start | bytes 1572872 | tf_op jit(solution)/shard_map/ppermute | solution.py:631
  6.1 29.8 %collective-permute-start.2 = (bf16[8,256,128]{2,1,0:T(8,128)(2,1)}, bf16[8,256,128]{2,1,0:T(8,128)(2,1)}, u32[]{:S(2)}, u32[]{:S(2)}) collective-permute-start(bf16[8,256,128]{2,1,0:T(8,128)(2,1)} %refs_0_.14), channel_id=1, source_target_pairs={{0,2},{3,1},{4,6},{7,5},{8,10},{11,9},{12,14},{15,13},{16,18},{19,... | collective-permute-start | bytes 1572872 | tf_op jit(solution)/shard_map/ppermute | solution.py:631
  13.3 8.6 %copy-start.6 = (s32[8,256]{1,0:T(8,128)S(1)}, s32[8,256]{1,0:T(8,128)}, u32[]{:S(2)}) copy-start(s32[8,256]{1,0:T(8,128)} %param.11) | copy-start | bytes 24580
  13.3 9.9 %copy-start.5 = (bf16[2,8,2048]{2,1,0:T(8,128)(2,1)S(1)}, bf16[2,8,2048]{2,1,0:T(8,128)(2,1)}, u32[]{:S(2)}) copy-start(bf16[2,8,2048]{2,1,0:T(8,128)(2,1)} %param.10) | copy-start | bytes 196612
  13.3 42.7 %collective-permute-start.10 = (bf16[4096,128]{1,0:T(8,128)(2,1)}, bf16[4096,128]{1,0:T(8,128)(2,1)}, u32[]{:S(2)}, u32[]{:S(2)}) collective-permute-start(bf16[4096,128]{1,0:T(8,128)(2,1)} %cut.7), channel_id=1, source_target_pairs={{1,0},{2,1},{3,2},{5,4},{6,5},{7,6},{9,8},{10,9},{11,10},{13,12},{... | collective-permute-start | bytes 3145736 | tf_op jit(solution)/shard_map/ppermute | solution.py:631
  16.8 40.4 %collective-permute-start.9 = (bf16[4096,128]{1,0:T(8,128)(2,1)}, bf16[4096,128]{1,0:T(8,128)(2,1)}, u32[]{:S(2)}, u32[]{:S(2)}) collective-permute-start(bf16[4096,128]{1,0:T(8,128)(2,1)} %cut.6), channel_id=1, source_target_pairs={{0,1},{1,2},{2,3},{4,5},{5,6},{6,7},{8,9},{9,10},{10,11},{12,13},{... | collective-permute-start | bytes 3145736 | tf_op jit(solution)/shard_map/ppermute | solution.py:631
  23.9 8.8 %copy-start.7 = (bf16[8,256]{1,0:T(8,128)(2,1)S(1)}, bf16[8,256]{1,0:T(8,128)(2,1)}, u32[]{:S(2)}) copy-start(bf16[8,256]{1,0:T(8,128)(2,1)} %param.9) | copy-start | bytes 12292
  23.9 8.8 %copy-start.8 = (s32[8]{0:T(128)S(1)}, s32[8]{0:T(128)}, u32[]{:S(2)}) copy-start(s32[8]{0:T(128)} %param.12) | copy-start | bytes 100
  34.6 33.5 %collective-permute-start.6 = (bf16[8,256,128]{2,1,0:T(8,128)(2,1)}, bf16[8,256,128]{2,1,0:T(8,128)(2,1)S(1)}, u32[]{:S(2)}, u32[]{:S(2)}) collective-permute-start(bf16[8,256,128]{2,1,0:T(8,128)(2,1)} %get-tuple-element.14.refs_0_), channel_id=1, source_target_pairs={{0,1},{1,2},{2,3},{4,5},{5,6},{6,7},{8,9},{9,10},{10,11},{12,13},{... | collective-permute-start | bytes 1572872 | tf_op jit(solution)/shard_map/ppermute | solution.py:631
  40.2 8.5 %collective-permute-start.3 = (bf16[3,4,256]{2,1,0:T(4,128)(2,1)S(1)}, bf16[3,4,256]{2,1,0:T(4,128)(2,1)S(1)}, u32[]{:S(2)}, u32[]{:S(2)}) collective-permute-start(bf16[3,4,256]{2,1,0:T(4,128)(2,1)S(1)} %get-tuple-element.21), channel_id=1, source_target_pairs={{0,4},{4,8},{8,12},{12,16},{16,20},{20,24},{24,28},{1,5},{5,9},{9,... | collective-permute-start | bytes 18440 | tf_op jit(solution)/shard_map/ppermute | solution.py:646
  45.3 4.9 %collective-permute-start.4 = (bf16[3,4,256]{2,1,0:T(4,128)(2,1)S(1)}, bf16[3,4,256]{2,1,0:T(4,128)(2,1)S(1)}, u32[]{:S(2)}, u32[]{:S(2)}) collective-permute-start(bf16[3,4,256]{2,1,0:T(4,128)(2,1)S(1)} %get-tuple-element.22), channel_id=1, source_target_pairs={{4,0},{8,4},{12,8},{16,12},{20,16},{24,20},{28,24},{5,1},{9,5},{13... | collective-permute-start | bytes 18440 | tf_op jit(solution)/shard_map/ppermute | solution.py:646
  48.7 19.4 %collective-permute-start.7 = (bf16[8,256,128]{2,1,0:T(8,128)(2,1)}, bf16[8,256,128]{2,1,0:T(8,128)(2,1)S(1)}, u32[]{:S(2)}, u32[]{:S(2)}) collective-permute-start(bf16[8,256,128]{2,1,0:T(8,128)(2,1)} %get-tuple-element.14.refs_0_), channel_id=1, source_target_pairs={{1,0},{2,1},{3,2},{5,4},{6,5},{7,6},{9,8},{10,9},{11,10},{13,12},{... | collective-permute-start | bytes 1572872 | tf_op jit(solution)/shard_map/ppermute | solution.py:631
  50.3 20.9 %collective-permute-start.8 = (bf16[8,256,128]{2,1,0:T(8,128)(2,1)}, bf16[8,256,128]{2,1,0:T(8,128)(2,1)S(1)}, u32[]{:S(2)}, u32[]{:S(2)}) collective-permute-start(bf16[8,256,128]{2,1,0:T(8,128)(2,1)} %get-tuple-element.14.refs_0_), channel_id=1, source_target_pairs={{0,2},{3,1},{4,6},{7,5},{8,10},{11,9},{12,14},{15,13},{16,18},{19,... | collective-permute-start | bytes 1572872 | tf_op jit(solution)/shard_map/ppermute | solution.py:631
  56.0 30.5 %collective-permute-start.5 = (bf16[2,8,256,128]{3,2,1,0:T(8,128)(2,1)}, bf16[2,8,256,128]{3,2,1,0:T(8,128)(2,1)}, u32[]{:S(2)}, u32[]{:S(2)}) collective-permute-start(bf16[2,8,256,128]{3,2,1,0:T(8,128)(2,1)} %relay.2.refs_1_.refs_3_), channel_id=1, source_target_pairs={{2,3},{1,0},{6,7},{5,4},{10,11},{9,8},{14,15},{13,12},{18,19},{17,... | collective-permute-start | bytes 3145736 | tf_op jit(solution)/shard_map/ppermute | solution.py:635
  68.1 3.0 %copy-start = (bf16[8,256,128]{2,1,0:T(8,128)(2,1)}, bf16[8,256,128]{2,1,0:T(8,128)(2,1)S(1)}, u32[]{:S(2)}) copy-start(bf16[8,256,128]{2,1,0:T(8,128)(2,1)S(1)} %collective-permute-done.6.refs_0_.refs_1_) | copy-start | bytes 1572868
  68.1 3.0 %copy-start.1 = (bf16[8,256,128]{2,1,0:T(8,128)(2,1)}, bf16[8,256,128]{2,1,0:T(8,128)(2,1)S(1)}, u32[]{:S(2)}) copy-start(bf16[8,256,128]{2,1,0:T(8,128)(2,1)S(1)} %collective-permute-done.7.refs_1_.refs_2_) | copy-start | bytes 1572868
  71.2 0.8 copy-start.2
  74.1 44.9 %collective-permute-start.11 = (bf16[2,8,256,128]{3,2,1,0:T(8,128)(2,1)}, bf16[2,8,256,128]{3,2,1,0:T(8,128)(2,1)}, u32[]{:S(2)}, u32[]{:S(2)}) collective-permute-start(bf16[2,8,256,128]{3,2,1,0:T(8,128)(2,1)} %relay.3.refs_5_.refs_1_), channel_id=1, source_target_pairs={{2,3},{1,0},{6,7},{5,4},{10,11},{9,8},{14,15},{13,12},{18,19},{17,... | collective-permute-start | bytes 3145736 | tf_op jit(solution)/shard_map/ppermute | solution.py:635
  77.6 41.4 %collective-permute-start.12 = (bf16[4096,128]{1,0:T(8,128)(2,1)}, bf16[4096,128]{1,0:T(8,128)(2,1)S(1)}, u32[]{:S(2)}, u32[]{:S(2)}) collective-permute-start(bf16[4096,128]{1,0:T(8,128)(2,1)} %cut.8), channel_id=1, source_target_pairs={{0,2},{3,1},{4,6},{7,5},{8,10},{11,9},{12,14},{15,13},{16,18},{19,... | collective-permute-start | bytes 3145736 | tf_op jit(solution)/shard_map/ppermute | solution.py:631
  90.5 28.5 %collective-permute-start.13 = (bf16[3,256,512]{2,1,0:T(8,128)(2,1)}, bf16[3,256,512]{2,1,0:T(8,128)(2,1)S(1)}, u32[]{:S(2)}, u32[]{:S(2)}) collective-permute-start(bf16[3,256,512]{2,1,0:T(8,128)(2,1)} %get-tuple-element.16), channel_id=1, source_target_pairs={{0,4},{4,8},{8,12},{12,16},{16,20},{20,24},{24,28},{1,5},{5,9},{9,... | collective-permute-start | bytes 2359304 | tf_op jit(solution)/shard_map/ppermute | solution.py:646
  96.0 23.1 %collective-permute-start.14 = (bf16[3,256,512]{2,1,0:T(8,128)(2,1)}, bf16[3,256,512]{2,1,0:T(8,128)(2,1)}, u32[]{:S(2)}, u32[]{:S(2)}) collective-permute-start(bf16[3,256,512]{2,1,0:T(8,128)(2,1)} %get-tuple-element.17), channel_id=1, source_target_pairs={{4,0},{8,4},{12,8},{16,12},{20,16},{24,20},{28,24},{5,1},{9,5},{13... | collective-permute-start | bytes 2359304 | tf_op jit(solution)/shard_map/ppermute | solution.py:646
  100.1 36.7 %collective-permute-start.17 = (bf16[4096,128]{1,0:T(8,128)(2,1)}, bf16[4096,128]{1,0:T(8,128)(2,1)}, u32[]{:S(2)}, u32[]{:S(2)}) collective-permute-start(bf16[4096,128]{1,0:T(8,128)(2,1)} %cut.9), channel_id=1, source_target_pairs={{0,3},{3,0},{4,7},{7,4},{8,11},{11,8},{12,15},{15,12},{16,19},{19,... | collective-permute-start | bytes 3145736 | tf_op jit(solution)/shard_map/ppermute | solution.py:631
  119.0 1.0 copy-start.3
  119.0 1.2 copy-start.4
  124.2 15.5 %collective-permute-start.15 = (bf16[3,256,512]{2,1,0:T(8,128)(2,1)}, bf16[3,256,512]{2,1,0:T(8,128)(2,1)S(1)}, u32[]{:S(2)}, u32[]{:S(2)}) collective-permute-start(bf16[3,256,512]{2,1,0:T(8,128)(2,1)} %get-tuple-element.18), channel_id=1, source_target_pairs={{0,4},{4,8},{8,12},{12,16},{16,20},{20,24},{24,28},{1,5},{5,9},{9,... | collective-permute-start | bytes 2359304 | tf_op jit(solution)/shard_map/ppermute | solution.py:646
  128.5 19.5 %collective-permute-start.16 = (bf16[3,256,512]{2,1,0:T(8,128)(2,1)}, bf16[3,256,512]{2,1,0:T(8,128)(2,1)S(1)}, u32[]{:S(2)}, u32[]{:S(2)}) collective-permute-start(bf16[3,256,512]{2,1,0:T(8,128)(2,1)} %get-tuple-element.19), channel_id=1, source_target_pairs={{4,0},{8,4},{12,8},{16,12},{20,16},{24,20},{28,24},{5,1},{9,5},{13... | collective-permute-start | bytes 2359304 | tf_op jit(solution)/shard_map/ppermute | solution.py:646
  132.3 19.2 %collective-permute-start.19 = (bf16[2048,128]{1,0:T(8,128)(2,1)}, bf16[2048,128]{1,0:T(8,128)(2,1)}, u32[]{:S(2)}, u32[]{:S(2)}) collective-permute-start(bf16[2048,128]{1,0:T(8,128)(2,1)} %cut.11), channel_id=1, source_target_pairs={{1,3},{2,0},{5,7},{6,4},{9,11},{10,8},{13,15},{14,12},{17,19},{18,... | collective-permute-start | bytes 1572872 | tf_op jit(solution)/shard_map/ppermute | solution.py:631
  135.5 26.4 %collective-permute-start.18 = (bf16[2048,128]{1,0:T(8,128)(2,1)}, bf16[2048,128]{1,0:T(8,128)(2,1)}, u32[]{:S(2)}, u32[]{:S(2)}) collective-permute-start(bf16[2048,128]{1,0:T(8,128)(2,1)} %cut.10), channel_id=1, source_target_pairs={{1,3},{2,0},{5,7},{6,4},{9,11},{10,8},{13,15},{14,12},{17,19},{18,... | collective-permute-start | bytes 1572872 | tf_op jit(solution)/shard_map/ppermute | solution.py:631
  139.7 8.4 %copy-start.9 = (bf16[3,256,512]{2,1,0:T(8,128)(2,1)}, bf16[3,256,512]{2,1,0:T(8,128)(2,1)S(1)}, u32[]{:S(2)}) copy-start(bf16[3,256,512]{2,1,0:T(8,128)(2,1)S(1)} %collective-permute-done.15.before_ref.refs_4_) | copy-start | bytes 2359300
  148.1 0.9 copy-start.10
